TPU v7x, 32 devices: a whole 2x2x4 slice. The times are simulated.
32 devices in a mesh: island: 2 (over x), dp: 2 (over y), expert: 8 (over z, core).
Axes of the slice: x: 2, y: 2, z: 4, core: 2. Of those that a mesh axis runs over, the one named last changes fastest.
Arguments:
- theta: bfloat16 [2, 8, 384, 2048], P('island', 'expert', 'dp'), may hold values from -7.5 to 7.5
- first_moment: bfloat16 [2, 8, 384, 2048], P('island', 'expert', 'dp'), may hold values from -0.119628906 to 0.119628906
- second_moment: bfloat16 [2, 8, 384, 2048], P('island', 'expert', 'dp'), may hold values from 9.9658966e-05 to 0.0099487305
- anchor: float32 [8, 384, 2048], P('expert', 'dp', 'island'), may hold values from -4.5 to 4.5
- momentum: float32 [8, 384, 2048], P('expert', 'dp', 'island'), may hold values from -1.8 to 1.8
- cotangent: bfloat16 [4096, 2048], P(('island', 'dp', 'expert')), may hold values from -6 to 6
- weights: float32 [4096, 8], P(('island', 'dp', 'expert')), may hold values from 0.05 to 0.3
- expert_ids: int32 [4096, 8], P(('island', 'dp', 'expert')), may hold values from 0 to 127, as said below
- expert_counts: int32 [32, 4], P(('island', 'dp', 'expert')), may hold values from 1 to 16, as said below
- hidden_saved: bfloat16 [2, 2, 8, 128, 384], P('island', 'dp', 'expert'), may hold values from -6 to 6
Outputs:
- anchor_new: float32 [8, 384, 2048], P('expert', 'dp', 'island')
- momentum_new: float32 [8, 384, 2048], P('expert', 'dp', 'island')
- d_hidden: bfloat16 [2, 2, 8, 128, 384], P('island', 'dp', 'expert')
Inputs may be any that keep to these rules, and one draw needn't show every extreme that they name: `expert_ids`: in each block of 128 rows a row's ids are distinct, every id below 4 is named by 1 to 16 pairs of the block, and those counts equal expert_counts of the block. expert_counts[b, e] is the number of pairs of block b naming expert e.
All inputs are finite; a program needn't handle non-finite values.
Results may differ from a plain program's by a relative error of at most 0.014.
Values may be sent and summed in bfloat16 or wider, within the bound.
No kernel may reach another device: no remote copies, remote signals or barrier semaphores. Data moves between devices by JAX's collectives and lax.ppermute only.
A program may use at most 64 MiB of HBM per device.

v0:
```python
import functools

import jax
import jax.numpy as jnp
from jax import lax
from jax.experimental import pallas as pl
from jax.experimental.pallas import tpu as pltpu
from jax.sharding import PartitionSpec as P

FF = 768
CAP = 16

beta_one = 0.9
beta_two = 0.95
adam_epsilon = 1e-08
inner_rate = 0.1
decay_rate = 0.1
outer_beta = 0.9
outer_rate = 0.7

VMEM = pl.BlockSpec(memory_space=pltpu.VMEM)
HBM = pl.BlockSpec(memory_space=pltpu.HBM)
PARAMS = pltpu.CompilerParams(vmem_limit_bytes=48 * 1024 * 1024)


PEAK = 1.15e15
MICROSECONDS = {
    "stage": 1.6,
    "split": 0.1,
    "assemble": 0.05,
    "rest": 0.05,
    "far_one": 0.1,
    "far_two": 0.3,
    "hidden_grad": 0.3,
    "near_update": 0.3,
    "outer_one": 1.1,
    "outer_two": 0.9,
}


def in_hbm(value):
    return pltpu.with_memory_space_constraint(value, pltpu.HBM)


def wrap(value, size):
    return lax.rem(value + size, size)


def target(place, step, size):
    return place ^ step if size & (size - 1) == 0 else (place + step) % size


def order(size):
    return sorted(range(size), key=lambda step: (step == 0, step != size // 2, -step))


def source(place, step, size):
    return place ^ step if size & (size - 1) == 0 else (place - step) % size


def cut(part):
    return part * 3 // 4 // 128 * 128


def pieces(n_island, width):
    part = width // n_island
    first = cut(part)
    island = lax.axis_index("island")
    order = [(shift, 0, first) for shift in range(1, n_island)]
    order += [(shift, first, part - first) for shift in range(1, n_island)]
    order += [(n_island, 0, part)]
    found, at = [], 0
    for shift, skip, size in order:
        column = lax.rem(island + shift, n_island) * part + skip
        found.append((slice(at, at + size), pl.ds(pl.multiple_of(column, 128), size)))
        at += size
    return found


def pack_body(experts, n_island, ids_hbm, weights_hbm, counts_hbm, cot_hbm, *refs):
    outs = refs[:experts]
    ids_ref, weights_ref, counts_ref, cot_ref, sems = refs[experts:]
    copies = [
        pltpu.make_async_copy(src, dst, sems.at[index])
        for index, (src, dst) in enumerate(
            [
                (ids_hbm, ids_ref),
                (weights_hbm, weights_ref),
                (counts_hbm, counts_ref),
                (cot_hbm, cot_ref),
            ]
        )
    ]
    for copy in copies:
        copy.start()
    width, tokens = ids_ref.shape
    rows = experts * CAP
    place = lax.div(lax.axis_index("expert"), 2)
    step = lax.broadcasted_iota(jnp.int32, (experts, CAP, tokens), 0).reshape(rows, tokens)
    expert = target(place, step, experts)
    rank = lax.broadcasted_iota(jnp.int32, (experts, CAP, tokens), 1).reshape(rows, tokens)
    earlier = (
        lax.broadcasted_iota(jnp.int32, (tokens, tokens), 0)
        < lax.broadcasted_iota(jnp.int32, (tokens, tokens), 1)
    )
    earlier = jnp.where(earlier, 1.0, 0.0).astype(jnp.bfloat16)
    for copy in copies[:3]:
        copy.wait()
    named = jnp.zeros((rows, tokens), jnp.float32)
    weight = jnp.zeros((rows, tokens), jnp.float32)
    for slot in range(width):
        hit = ids_ref[slot : slot + 1, :] == expert
        named = jnp.where(hit, 1.0, named)
        weight = jnp.where(hit, weights_ref[slot : slot + 1, :], weight)
    limit = jnp.zeros((rows, tokens), jnp.int32)
    for index in range(experts):
        limit = jnp.where(expert == index, counts_ref[:, index : index + 1], limit)
    found = jnp.dot(named.astype(jnp.bfloat16), earlier, preferred_element_type=jnp.float32)
    found = found.astype(jnp.int32)
    picked = (named > 0.0) & (found < limit) & (found == rank)
    pick = jnp.where(picked, 1.0, 0.0)
    scale = jnp.sum(pick * weight, axis=1, keepdims=True)
    pick = pick.astype(jnp.bfloat16)
    copies[3].wait()
    for at, columns in pieces(n_island, cot_ref.shape[1]):
        gathered = jnp.dot(pick, cot_ref[:, columns], preferred_element_type=jnp.float32)
        packed = (gathered * scale).astype(jnp.bfloat16)
        for index, out in enumerate(outs):
            out[:, at] = packed[index * CAP : (index + 1) * CAP]


def pack_rows(cotangent, weights, expert_ids, counts, n_island):
    experts = counts.shape[1]
    ins = [expert_ids.T, weights.T, counts, cotangent]
    return pl.pallas_call(
        functools.partial(pack_body, experts, n_island),
        out_shape=[jax.ShapeDtypeStruct((CAP, cotangent.shape[1]), jnp.bfloat16)] * experts,
        in_specs=[HBM] * 4,
        out_specs=[VMEM] * experts,
        scratch_shapes=[
            pltpu.VMEM(expert_ids.shape[::-1], jnp.int32),
            pltpu.VMEM(weights.shape[::-1], jnp.float32),
            pltpu.VMEM(counts.shape, jnp.int32),
            pltpu.VMEM(cotangent.shape, jnp.bfloat16),
            pltpu.SemaphoreType.DMA((4,)),
        ],
        compiler_params=PARAMS,
        name="pack",
    )(*[in_hbm(value) for value in ins])


def adam(product, first, second, theta):
    scale = FF ** (-0.5)
    wide = theta.astype(jnp.float32)
    first_new = (inner_rate * beta_one) * first.astype(jnp.float32)
    first_new = first_new + (inner_rate * (1.0 - beta_one) * scale) * product
    second_new = beta_two * second.astype(jnp.float32)
    second_new = second_new + ((1.0 - beta_two) * scale * scale) * (product * product)
    step_size = first_new / (jnp.sqrt(second_new) + adam_epsilon)
    return ((1.0 - inner_rate * decay_rate) * wide - step_size).astype(jnp.bfloat16)


def assemble_body(pairs, *refs):
    blocks, (one_ref, two_ref) = refs[:pairs], refs[-2:]
    split = one_ref.shape[1]
    for index, block in enumerate(blocks):
        rows = slice(index * CAP, (index + 1) * CAP)
        one_ref[rows, :] = block[:, :split]
        two_ref[rows, :] = block[:, split:]


def rest_body(two_ref, *refs):
    refs[-1][...] = two_ref[...]


def stage_body(*refs):
    states, copied, sems = refs[:3], refs[4:7], refs[7]
    copies = [
        pltpu.make_async_copy(src, dst, sems.at[index])
        for index, (src, dst) in enumerate(zip(states, copied))
    ]
    for copy in copies:
        copy.start()
    for copy in copies:
        copy.wait()


def split_body(n_dp, saved_ref, _, *refs):
    *outs, scratch = refs
    units = outs[0].shape[0]
    scratch[...] = saved_ref[...].astype(jnp.float32).T
    for shift, out in enumerate(outs):
        row = pl.multiple_of(lax.rem(lax.axis_index("dp") + shift, n_dp) * units, 8)
        out[...] = scratch[pl.ds(row, units), :].astype(jnp.bfloat16)


def gather_slots(n_dp, pairs, quarters, slots_ref):
    data, position = lax.axis_index("dp"), lax.axis_index("expert")
    core = lax.rem(position, 2)
    place = lax.div(position, 2)
    length = 2 * pairs * CAP
    for shift in range(n_dp):
        group = wrap(data - shift, n_dp)
        for flip in range(2):
            side = core if flip == 0 else 1 - core
            block = quarters[2 * shift + flip]
            for k in range(pairs):
                at = order(pairs).index(k) * CAP
                row = group * length + (2 * source(place, k, pairs) + side) * CAP
                row = pl.multiple_of(row, CAP)
                slots_ref[pl.ds(row, CAP), :] = block[at : at + CAP, :]


def update(left, slots, state_refs, columns):
    product = jnp.dot(left, slots, preferred_element_type=jnp.float32)
    theta, first, second = (ref[:, columns] for ref in state_refs)
    return adam(product, first, second, theta)


def one_body(n_dp, n_island, pairs, *refs):
    quarters = refs[: 2 * n_dp]
    saved = refs[2 * n_dp : 3 * n_dp]
    state_refs = refs[3 * n_dp : 3 * n_dp + 3]
    *outs, slots_ref, left_ref = refs[3 * n_dp + 3 :]
    length = saved[0].shape[1]
    for shift, value in enumerate(saved):
        column = pl.multiple_of(wrap(lax.axis_index("dp") - shift, n_dp) * length, 128)
        left_ref[:, pl.ds(column, length)] = value[...]
    gather_slots(n_dp, pairs, quarters, slots_ref)
    places = pieces(n_island, state_refs[0].shape[1])
    for out, (at, columns) in zip(outs, places):
        out[...] = update(left_ref[...], slots_ref[:, at], state_refs, columns)


def two_body(n_dp, n_island, pairs, *refs):
    quarters = refs[: 2 * n_dp]
    left_ref, *state_refs = refs[2 * n_dp : 2 * n_dp + 4]
    *outs, slots_ref = refs[2 * n_dp + 4 :]
    width = state_refs[0].shape[1]
    first = width - slots_ref.shape[1]
    gather_slots(n_dp, pairs, quarters, slots_ref)
    places = pieces(n_island, width)[n_island - 1 :]
    for out, (at, columns) in zip(outs, places):
        slots = slots_ref[:, at.start - first : at.stop - first]
        out[...] = update(left_ref[...], slots, state_refs, columns)


def hidden_body(n_dp, n_island, one_ref, two_ref, theta_ref, *outs):
    data = lax.axis_index("dp")
    split = one_ref.shape[1]
    length = one_ref.shape[0] // n_dp
    total = None
    for at, columns in pieces(n_island, theta_ref.shape[1]):
        in_one = at.stop <= split
        slots = one_ref[:, at] if in_one else two_ref[:, at.start - split : at.stop - split]
        value = lax.dot_general(
            theta_ref[:, columns],
            slots,
            (((1,), (1,)), ((), ())),
            preferred_element_type=jnp.float32,
        )
        total = value if total is None else total + value
    hidden = (FF ** (-0.5) * total).astype(jnp.bfloat16)
    for shift, out in enumerate(outs):
        for group in range(n_dp):

            @pl.when(lax.rem(data + shift, n_dp) == group)
            def _():
                out[...] = hidden[:, group * length : (group + 1) * length]


def near_body(slots_ref, left_ref, *refs):
    *state_refs, own_ref = refs
    part = own_ref.shape[1]
    columns = pl.ds(pl.multiple_of(lax.axis_index("island") * part, 128), part)
    slots = slots_ref[:, slots_ref.shape[1] - part :]
    own_ref[...] = update(left_ref[...], slots, state_refs, columns)


def outer_step(columns, anchor_ref, momentum_ref, own_ref, theirs, results, outs, sems):
    n_island = len(theirs) + 1
    rows = anchor_ref.shape[0]
    steps = 2 if rows % 16 == 0 else 1
    copies = []
    for step in range(steps):
        at = slice(step * (rows // steps), (step + 1) * (rows // steps))
        total = own_ref[at, columns].astype(jnp.float32)
        for theta in theirs:
            total = total + theta[at, :].astype(jnp.float32)
        anchor = anchor_ref[at, columns]
        mean_delta = anchor - total * (1.0 / n_island)
        momentum_new = outer_beta * momentum_ref[at, columns] + mean_delta
        results[1][at, :] = momentum_new
        results[0][at, :] = anchor - outer_rate * (mean_delta + outer_beta * momentum_new)
        for index in range(2):
            copies.append(
                pltpu.make_async_copy(
                    results[index].at[at, :], outs[index].at[at, columns], sems.at[index, step]
                )
            )
            copies[-1].start()
    return copies


def outer_one_body(n_island, n_dp, anchor_ref, momentum_ref, own_ref, *refs):
    theirs, refs = refs[: n_island - 1], refs[n_island - 1 :]
    hidden, refs = refs[:n_dp], refs[n_dp:]
    *outs, hidden_out = refs[:3]
    *results, hidden_ref, scratch, sems = refs[3:]
    data = lax.axis_index("dp")
    units = hidden[0].shape[0]
    for shift, value in enumerate(hidden):
        row = pl.multiple_of(wrap(data - shift, n_dp) * units, 8)
        scratch[pl.ds(row, units), :] = value[...].astype(jnp.float32)
    columns = slice(0, results[0].shape[1])
    copies = outer_step(columns, anchor_ref, momentum_ref, own_ref, theirs, results, outs, sems)
    hidden_ref[...] = scratch[...].T.astype(jnp.bfloat16)
    copies.append(pltpu.make_async_copy(hidden_ref, hidden_out, sems.at[2, 0]))
    copies[-1].start()
    for copy in copies:
        copy.wait()


def outer_two_body(n_island, _, __, anchor_ref, momentum_ref, own_ref, *refs):
    theirs, outs = refs[: n_island - 1], refs[n_island - 1 : n_island + 1]
    *results, sems = refs[n_island + 1 :]
    part = anchor_ref.shape[1]
    columns = slice(part - results[0].shape[1], part)
    for copy in outer_step(columns, anchor_ref, momentum_ref, own_ref, theirs, results, outs, sems):
        copy.wait()


def call(body, out_shape, ins, name, scratch=(), in_specs=None, out_specs=None, aliases=None):
    flops = int(MICROSECONDS[name] * PEAK / 1e6)
    cost = pl.CostEstimate(flops=flops, transcendentals=0, bytes_accessed=0)
    return pl.pallas_call(
        body,
        out_shape=out_shape,
        in_specs=in_specs or [VMEM] * len(ins),
        out_specs=out_specs or [VMEM] * len(out_shape),
        scratch_shapes=list(scratch),
        input_output_aliases=aliases or {},
        cost_estimate=cost,
        compiler_params=PARAMS,
        name=name,
    )(*ins)


def per_device(
    theta,
    first_moment,
    second_moment,
    anchor,
    momentum,
    cotangent,
    weights,
    expert_ids,
    expert_counts,
    hidden_saved,
):
    n_island, n_dp, n_expert = (lax.axis_size(name) for name in ("island", "dp", "expert"))
    pairs = n_expert // 2
    units, width = theta.shape[2:]
    length, full_units = hidden_saved.shape[3:]
    part = width // n_island
    first = cut(part)
    split = (n_island - 1) * first
    bf16 = functools.partial(jax.ShapeDtypeStruct, dtype=jnp.bfloat16)

    def ring(value, name, size, shift):
        return lax.ppermute(value, name, [(k, (k + shift) % size) for k in range(size)])

    blocks = list(pack_rows(cotangent, weights, expert_ids, expert_counts, n_island))
    arrived = []
    for k in order(pairs)[:-1]:
        perm = [(2 * z + c, 2 * target(z, k, pairs) + c) for z in range(pairs) for c in range(2)]
        arrived.append(lax.ppermute(blocks[k], "expert", perm))
    saved = hidden_saved.reshape(length, full_units)
    saved_all = call(
        functools.partial(split_body, n_dp),
        [bf16((units, length))] * n_dp,
        [saved, blocks[0]],
        "split",
        [pltpu.VMEM((full_units, length), jnp.float32)],
    )
    saved_all = [ring(saved_all[s], "dp", n_dp, s) if s else saved_all[0] for s in range(n_dp)]
    arrived.append(blocks[0])
    one_mine, two_mine = call(
        functools.partial(assemble_body, pairs),
        [bf16((pairs * CAP, columns)) for columns in (split, width - split)],
        arrived + saved_all[1:],
        "assemble",
    )
    swap = [(j, j ^ 1) for j in range(n_expert)]

    def spread(mine, after=None):
        quarters = [mine, lax.ppermute(mine, "expert", swap)]
        for shift in range(1, n_dp):
            value = ring(mine, "dp", n_dp, shift)
            if after is not None:
                value, _ = lax.optimization_barrier((value, after))
            quarters += [value, lax.ppermute(value, "expert", swap)]
        return quarters

    one_quarters = spread(one_mine)
    states = [in_hbm(value.reshape(units, width)) for value in (theta, first_moment, second_moment)]
    states = call(
        stage_body,
        [bf16((units, width))] * 3,
        states + [one_mine],
        "stage",
        [pltpu.SemaphoreType.DMA((3,))],
        in_specs=[HBM] * 3 + [VMEM],
    )
    (two_mine,) = call(
        rest_body,
        [bf16((pairs * CAP, width - split))],
        [two_mine, one_quarters[1], *states],
        "rest",
    )
    *one, one_slots, left = call(
        functools.partial(one_body, n_dp, n_island, pairs),
        [bf16((units, first))] * (n_island - 1)
        + [bf16((n_dp * length, split)), bf16((units, n_dp * length))],
        one_quarters + saved_all + list(states),
        "far_one",
    )
    theirs = [ring(value, "island", n_island, shift + 1) for shift, value in enumerate(one)]
    two_quarters = spread(two_mine, left)
    *two, two_slots = call(
        functools.partial(two_body, n_dp, n_island, pairs),
        [bf16((units, part - first))] * (n_island - 1)
        + [bf16((n_dp * length, width - split))],
        two_quarters + [left, *states],
        "far_two",
    )
    theirs += [ring(value, "island", n_island, shift + 1) for shift, value in enumerate(two)]
    hidden = call(
        functools.partial(hidden_body, n_dp, n_island),
        [bf16((units, length))] * n_dp,
        [one_slots, two_slots, states[0]],
        "hidden_grad",
    )
    hidden = [hidden[0]] + [ring(hidden[s], "dp", n_dp, s) for s in range(1, n_dp)]
    (own,) = call(near_body, [bf16((units, part))], [two_slots, left, *states], "near_update")
    outer = [anchor.reshape(units, part), momentum.reshape(units, part), own]
    outer_type = jax.ShapeDtypeStruct((units, part), jnp.float32)
    *begun, d_hidden = call(
        functools.partial(outer_one_body, n_island, n_dp),
        [outer_type, outer_type, bf16((length, full_units))],
        outer + theirs[: n_island - 1] + hidden,
        "outer_one",
        [pltpu.VMEM((units, first), jnp.float32)] * 2
        + [
            pltpu.VMEM((length, full_units), jnp.bfloat16),
            pltpu.VMEM((full_units, length), jnp.float32),
            pltpu.SemaphoreType.DMA((3, 2)),
        ],
        out_specs=[HBM, HBM, HBM],
    )
    ins = [*begun, *outer, *theirs[n_island - 1 :]]
    anchor_new, momentum_new = call(
        functools.partial(outer_two_body, n_island),
        [outer_type, outer_type],
        ins,
        "outer_two",
        [pltpu.VMEM((units, part - first), jnp.float32)] * 2 + [pltpu.SemaphoreType.DMA((2, 2))],
        in_specs=[HBM, HBM] + [VMEM] * (len(ins) - 2),
        out_specs=[HBM, HBM],
        aliases={0: 0, 1: 1},
    )
    return (
        anchor_new.reshape(anchor.shape),
        momentum_new.reshape(momentum.shape),
        d_hidden.reshape(hidden_saved.shape),
    )


def solution(mesh):
    return jax.shard_map(
        per_device,
        mesh=mesh,
        in_specs=(
            P("island", "expert", "dp", None),
            P("island", "expert", "dp", None),
            P("island", "expert", "dp", None),
            P("expert", "dp", "island"),
            P("expert", "dp", "island"),
            P(("island", "dp", "expert"), None),
            P(("island", "dp", "expert"), None),
            P(("island", "dp", "expert"), None),
            P(("island", "dp", "expert"), None),
            P("island", "dp", "expert", None, None),
        ),
        out_specs=(
            P("expert", "dp", "island"),
            P("expert", "dp", "island"),
            P("island", "dp", "expert", None, None),
        ),
        check_vma=False,
    )
```

profile of v0, /device:TPU:0, one launch (start us, length us, event | category | flops | bytes accessed | tf_op | source)
XLA Modules:
  0.0 31.1 jit_solution(8553137207241806401)
XLA Ops:
  0.6 0.0 copy-start.2
  0.6 1.4 %pack.1 = (bf16[16,2048]{1,0:T(8,128)(2,1)S(1)}, bf16[16,2048]{1,0:T(8,128)(2,1)S(1)}, bf16[16,2048]{1,0:T(8,128)(2,1)S(1)}, bf16[16,2048]{1,0:T(8,128)(2,1)S(1)}) custom-call(s32[8,128]{1,0:T(8,128)} %bitcast.16, f32[8,128]{1,0:T(8,128)} %bitcast.17, s32[1,4]{1,0:T(1,128)} %counts_hbm.1, bf16[128,2048]{1,0:T(8,128)(2,1)} %cot_hbm.1), custom_call_target="tpu_custom_call" | custom-call | tf_op jit(solution)/shard_map/pack/pallas_call | solution.py:135
  2.0 4.1 %collective-permute-start = (bf16[16,2048]{1,0:T(8,128)(2,1)S(1)}, bf16[16,2048]{1,0:T(8,128)(2,1)S(1)}, u32[]{:S(2)}, u32[]{:S(2)}) collective-permute-start(bf16[16,2048]{1,0:T(8,128)(2,1)S(1)} %get-tuple-element.27), channel_id=1, source_target_pairs={{0,4},{1,5},{2,6},{3,7},{4,0},{5,1},{6,2},{7,3},{8,12},{9,13},{10,... | collective-permute-start | bytes 196616 | tf_op jit(solution)/shard_map/ppermute | solution.py:377
  6.1 1.3 %collective-permute-start.1 = (bf16[16,2048]{1,0:T(8,128)(2,1)S(1)}, bf16[16,2048]{1,0:T(8,128)(2,1)S(1)}, u32[]{:S(2)}, u32[]{:S(2)}) collective-permute-start(bf16[16,2048]{1,0:T(8,128)(2,1)S(1)} %get-tuple-element.28), channel_id=1, source_target_pairs={{0,6},{1,7},{2,4},{3,5},{4,2},{5,3},{6,0},{7,1},{8,14},{9,15},{10,... | collective-permute-start | bytes 196616 | tf_op jit(solution)/shard_map/ppermute | solution.py:377
  7.5 0.2 collective-permute-start.2
  7.7 0.0 copy-done.2
  7.7 0.1 split.1
  7.9 1.6 %collective-permute-start.3 = (bf16[192,128]{1,0:T(8,128)(2,1)S(1)}, bf16[192,128]{1,0:T(8,128)(2,1)S(1)}, u32[]{:S(2)}, u32[]{:S(2)}) collective-permute-start(bf16[192,128]{1,0:T(8,128)(2,1)S(1)} %get-tuple-element.31), channel_id=1, source_target_pairs={{0,8},{8,0},{1,9},{9,1},{2,10},{10,2},{3,11},{11,3},{4,12},{12,4},... | collective-permute-start | bytes 147464 | tf_op jit(solution)/shard_map/ppermute | solution.py:371
  9.4 2.6 %collective-permute-done.3.refs_4_.refs_5_ = bf16[192,128]{1,0:T(8,128)(2,1)S(1)} collective-permute-done((bf16[192,128]{1,0:T(8,128)(2,1)S(1)}, bf16[192,128]{1,0:T(8,128)(2,1)S(1)}, u32[]{:S(2)}, u32[]{:S(2)}) %collective-permute-start.3) | collective-permute-done | bytes 49184 | tf_op jit(solution)/shard_map/ppermute | solution.py:371
  12.0 0.0 collective-permute-done.refs_0_
  12.0 0.4 %collective-permute-done.1.refs_1_ = bf16[16,2048]{1,0:T(8,128)(2,1)S(1)} collective-permute-done((bf16[16,2048]{1,0:T(8,128)(2,1)S(1)}, bf16[16,2048]{1,0:T(8,128)(2,1)S(1)}, u32[]{:S(2)}, u32[]{:S(2)}) %collective-permute-start.1) | collective-permute-done | bytes 65568 | tf_op jit(solution)/shard_map/ppermute | solution.py:377
  12.4 0.1 collective-permute-done.2.refs_2_
  12.5 1.6 %collective-permute-start.7 = (bf16[64,768]{1,0:T(8,128)(2,1)S(1)}, bf16[64,768]{1,0:T(8,128)(2,1)S(1)}, u32[]{:S(2)}, u32[]{:S(2)}) collective-permute-start(bf16[64,768]{1,0:T(8,128)(2,1)S(1)} %get-tuple-element.33.refs_3_.refs_0_), channel_id=1, source_target_pairs={{0,8},{8,0},{1,9},{9,1},{2,10},{10,2},{3,11},{11,3},{4,12},{12,4},... | collective-permute-start | bytes 294920 | tf_op jit(solution)/shard_map/ppermute | solution.py:371
  14.1 0.0 collective-permute-start.4
  14.1 1.6 %stage.1 = (bf16[192,2048]{1,0:T(8,128)(2,1)S(1)}, bf16[192,2048]{1,0:T(8,128)(2,1)S(1)}, bf16[192,2048]{1,0:T(8,128)(2,1)S(1)}) custom-call(bf16[192,2048]{1,0:T(8,128)(2,1)} %bitcast.18, bf16[192,2048]{1,0:T(8,128)(2,1)} %bitcast.19, bf16[192,2048]{1,0:T(8,128)(2,1)} %bitcast.20, bf16[64,768]{1,0:T(8,128)(2,1)S(1)} %get-tuple-element.33.refs_3_.refs_0_), custom_call_target="tpu_custom_call" | custom-call | flops 1840000000 | tf_op jit(solution)/shard_map/stage/pallas_call | solution.py:336
  15.7 0.0 collective-permute-done.4.refs_0_.refs_1_
  15.7 0.6 %collective-permute-start.6 = (bf16[64,1280]{1,0:T(8,128)(2,1)S(1)}, bf16[64,1280]{1,0:T(8,128)(2,1)S(1)}, u32[]{:S(2)}, u32[]{:S(2)}) collective-permute-start(bf16[64,1280]{1,0:T(8,128)(2,1)S(1)} %rest.1.refs_0_), channel_id=1, source_target_pairs={{0,8},{8,0},{1,9},{9,1},{2,10},{10,2},{3,11},{11,3},{4,12},{12,4},... | collective-permute-start | bytes 491528 | tf_op jit(solution)/shard_map/ppermute | solution.py:371
  16.3 0.8 %collective-permute-done.7.refs_2_ = bf16[64,768]{1,0:T(8,128)(2,1)S(1)} collective-permute-done((bf16[64,768]{1,0:T(8,128)(2,1)S(1)}, bf16[64,768]{1,0:T(8,128)(2,1)S(1)}, u32[]{:S(2)}, u32[]{:S(2)}) %collective-permute-start.7) | collective-permute-done | bytes 98336 | tf_op jit(solution)/shard_map/ppermute | solution.py:371
  17.2 0.0 collective-permute-start.8
  17.2 1.3 %collective-permute-done.8.refs_3_ = bf16[64,768]{1,0:T(8,128)(2,1)S(1)} collective-permute-done((bf16[64,768]{1,0:T(8,128)(2,1)S(1)}, bf16[64,768]{1,0:T(8,128)(2,1)S(1)}, u32[]{:S(2)}, u32[]{:S(2)}) %collective-permute-start.8) | collective-permute-done | bytes 98336 | tf_op jit(solution)/shard_map/ppermute | solution.py:402
  18.5 0.6 %far_one.1 = (bf16[192,768]{1,0:T(8,128)(2,1)S(1)}, bf16[256,768]{1,0:T(8,128)(2,1)S(1)}, bf16[192,256]{1,0:T(8,128)(2,1)S(1)}) custom-call(bf16[64,768]{1,0:T(8,128)(2,1)S(1)} %get-tuple-element.33.refs_3_.refs_0_, bf16[64,768]{1,0:T(8,128)(2,1)S(1)} %collective-permute-done.4.refs_0_.refs_1_, bf16[64,768]{1,0:T(8,128)(2,1)S(1)} %collective-permute-done.7.refs_2_, ...), custom_call_target="tpu_custom_call" | custom-call | flops 115000000 | tf_op jit(solution)/shard_map/far_one/pallas_call | solution.py:336
  19.1 1.6 %collective-permute-start.10 = (bf16[192,768]{1,0:T(8,128)(2,1)S(1)}, bf16[192,768]{1,0:T(8,128)(2,1)S(1)}, u32[]{:S(2)}, u32[]{:S(2)}) collective-permute-start(bf16[192,768]{1,0:T(8,128)(2,1)S(1)} %get-tuple-element.41), channel_id=1, source_target_pairs={{0,16},{16,0},{1,17},{17,1},{2,18},{18,2},{3,19},{19,3},{4,20},{20... | collective-permute-start | bytes 884744 | tf_op jit(solution)/shard_map/ppermute | solution.py:371
  20.7 0.0 collective-permute-start.5
  20.7 1.8 %collective-permute-done.6.refs_2_ = bf16[64,1280]{1,0:T(8,128)(2,1)S(1)} collective-permute-done((bf16[64,1280]{1,0:T(8,128)(2,1)S(1)}, bf16[64,1280]{1,0:T(8,128)(2,1)S(1)}, u32[]{:S(2)}, u32[]{:S(2)}) %collective-permute-start.6) | collective-permute-done | bytes 163872 | tf_op jit(solution)/shard_map/ppermute | solution.py:371
  22.4 0.0 collective-permute-start.9
  22.4 0.0 collective-permute-done.5.refs_1_
  22.4 1.4 %collective-permute-done.9.refs_3_ = bf16[64,1280]{1,0:T(8,128)(2,1)S(1)} collective-permute-done((bf16[64,1280]{1,0:T(8,128)(2,1)S(1)}, bf16[64,1280]{1,0:T(8,128)(2,1)S(1)}, u32[]{:S(2)}, u32[]{:S(2)}) %collective-permute-start.9) | collective-permute-done | bytes 163872 | tf_op jit(solution)/shard_map/ppermute | solution.py:402
  23.8 0.3 %far_two.1 = (bf16[192,256]{1,0:T(8,128)(2,1)S(1)}, bf16[256,1280]{1,0:T(8,128)(2,1)S(1)}) custom-call(bf16[64,1280]{1,0:T(8,128)(2,1)S(1)} %rest.1.refs_0_, bf16[64,1280]{1,0:T(8,128)(2,1)S(1)} %collective-permute-done.5.refs_1_, bf16[64,1280]{1,0:T(8,128)(2,1)S(1)} %collective-permute-done.6.refs_2_, bf16[64,1280]{1,0:T(8,128)(2,1)S(1)} %collective-permute-done.9.refs_3_, ...), custom_call_target="tpu_custom_call" | custom-call | flops 345000000 | tf_op jit(solution)/shard_map/far_two/pallas_call | solution.py:336
  24.2 0.5 %hidden_grad.1 = (bf16[192,128]{1,0:T(8,128)(2,1)S(1)}, bf16[192,128]{1,0:T(8,128)(2,1)S(1)}) custom-call(bf16[256,768]{1,0:T(8,128)(2,1)S(1)} %get-tuple-element.42.one_ref, bf16[256,1280]{1,0:T(8,128)(2,1)S(1)} %get-tuple-element.40.slots_ref.two_ref, bf16[192,2048]{1,0:T(8,128)(2,1)S(1)} %get-tuple-element.34.refs_1_.refs_6_.refs_5_.refs_0_.theta_ref), custom_call_target="tpu_custom_call" | custom-call | flops 345000000 | tf_op jit(solution)/shard_map/hidden_grad/pallas_call | solution.py:336
  24.7 0.6 %collective-permute-start.11 = (bf16[192,128]{1,0:T(8,128)(2,1)S(1)}, bf16[192,128]{1,0:T(8,128)(2,1)S(1)}, u32[]{:S(2)}, u32[]{:S(2)}) collective-permute-start(bf16[192,128]{1,0:T(8,128)(2,1)S(1)} %get-tuple-element.44), channel_id=1, source_target_pairs={{0,8},{8,0},{1,9},{9,1},{2,10},{10,2},{3,11},{11,3},{4,12},{12,4},... | collective-permute-start | bytes 147464 | tf_op jit(solution)/shard_map/ppermute | solution.py:371
  25.3 0.0 copy-start
  25.3 0.0 copy-start.1
  25.3 1.5 %collective-permute-start.12 = (bf16[192,256]{1,0:T(8,128)(2,1)S(1)}, bf16[192,256]{1,0:T(8,128)(2,1)S(1)}, u32[]{:S(2)}, u32[]{:S(2)}) collective-permute-start(bf16[192,256]{1,0:T(8,128)(2,1)S(1)} %get-tuple-element.47), channel_id=1, source_target_pairs={{0,16},{16,0},{1,17},{17,1},{2,18},{18,2},{3,19},{19,3},{4,20},{20... | collective-permute-start | bytes 294920 | tf_op jit(solution)/shard_map/ppermute | solution.py:371
  26.8 0.7 %near_update.1.own_ref = bf16[192,1024]{1,0:T(8,128)(2,1)S(1)} custom-call(bf16[256,1280]{1,0:T(8,128)(2,1)S(1)} %get-tuple-element.40.slots_ref.two_ref, bf16[192,256]{1,0:T(8,128)(2,1)S(1)} %get-tuple-element.38.refs_4_.left_ref, bf16[192,2048]{1,0:T(8,128)(2,1)S(1)} %get-tuple-element.34.refs_1_.refs_6_.refs_5_.refs_0_.theta_ref, ...), custom_call_target="tpu_custom_call" | custom-call | flops 345000000 | tf_op jit(solution)/shard_map/near_update/pallas_call | solution.py:336
  27.5 1.4 %collective-permute-done.11.refs_2_ = bf16[192,128]{1,0:T(8,128)(2,1)S(1)} collective-permute-done((bf16[192,128]{1,0:T(8,128)(2,1)S(1)}, bf16[192,128]{1,0:T(8,128)(2,1)S(1)}, u32[]{:S(2)}, u32[]{:S(2)}) %collective-permute-start.11) | collective-permute-done | bytes 49184 | tf_op jit(solution)/shard_map/ppermute | solution.py:371
  28.8 0.0 collective-permute-done.10.refs_0_
  28.8 0.0 copy-done
  28.9 0.0 copy-done.1
  28.9 1.3 %outer_one.1 = (f32[192,1024]{1,0:T(8,128)}, f32[192,1024]{1,0:T(8,128)}, bf16[128,384]{1,0:T(8,128)(2,1)}) custom-call(f32[192,1024]{1,0:T(8,128)S(1)} %bitcast.11, f32[192,1024]{1,0:T(8,128)S(1)} %bitcast.13, bf16[192,1024]{1,0:T(8,128)(2,1)S(1)} %near_update.1.own_ref, bf16[192,768]{1,0:T(8,128)(2,1)S(1)} %collective-permute-done.10.refs_0_, ...), custom_call_target="tpu_custom_call" | custom-call | flops 1264999936 | tf_op jit(solution)/shard_map/outer_one/pallas_call | solution.py:336
  30.2 0.2 collective-permute-done.12.refs_0_
  30.3 0.8 %outer_two.1 = (f32[192,1024]{1,0:T(8,128)}, f32[192,1024]{1,0:T(8,128)}) custom-call(f32[192,1024]{1,0:T(8,128)} %get-tuple-element.45._, f32[192,1024]{1,0:T(8,128)} %get-tuple-element.46.__, f32[192,1024]{1,0:T(8,128)S(1)} %bitcast.12, f32[192,1024]{1,0:T(8,128)S(1)} %bitcast.14, ...), custom_call_target="tpu_custom_call", output_to_operand_aliasing={{0}: (0, {}), {1}: (1, {})} | custom-call | flops 1035000000 | tf_op jit(solution)/shard_map/outer_two/pallas_call | solution.py:336
  (2 shorter events, 0.0 us)
Async XLA Ops:
  0.6 7.1 %copy-start.2 = (bf16[1,1,1,128,384]{4,3,2,1,0:T(8,128)(2,1)S(1)}, bf16[1,1,1,128,384]{4,3,2,1,0:T(8,128)(2,1)}, u32[]{:S(2)}) copy-start(bf16[1,1,1,128,384]{4,3,2,1,0:T(8,128)(2,1)} %param.19) | copy-start | bytes 294916
  2.0 10.0 %collective-permute-start = (bf16[16,2048]{1,0:T(8,128)(2,1)S(1)}, bf16[16,2048]{1,0:T(8,128)(2,1)S(1)}, u32[]{:S(2)}, u32[]{:S(2)}) collective-permute-start(bf16[16,2048]{1,0:T(8,128)(2,1)S(1)} %get-tuple-element.27), channel_id=1, source_target_pairs={{0,4},{1,5},{2,6},{3,7},{4,0},{5,1},{6,2},{7,3},{8,12},{9,13},{10,... | collective-permute-start | bytes 196616 | tf_op jit(solution)/shard_map/ppermute | solution.py:377
  6.1 6.2 %collective-permute-start.1 = (bf16[16,2048]{1,0:T(8,128)(2,1)S(1)}, bf16[16,2048]{1,0:T(8,128)(2,1)S(1)}, u32[]{:S(2)}, u32[]{:S(2)}) collective-permute-start(bf16[16,2048]{1,0:T(8,128)(2,1)S(1)} %get-tuple-element.28), channel_id=1, source_target_pairs={{0,6},{1,7},{2,4},{3,5},{4,2},{5,3},{6,0},{7,1},{8,14},{9,15},{10,... | collective-permute-start | bytes 196616 | tf_op jit(solution)/shard_map/ppermute | solution.py:377
  7.5 5.0 %collective-permute-start.2 = (bf16[16,2048]{1,0:T(8,128)(2,1)S(1)}, bf16[16,2048]{1,0:T(8,128)(2,1)S(1)}, u32[]{:S(2)}, u32[]{:S(2)}) collective-permute-start(bf16[16,2048]{1,0:T(8,128)(2,1)S(1)} %get-tuple-element.29), channel_id=1, source_target_pairs={{0,2},{1,3},{2,0},{3,1},{4,6},{5,7},{6,4},{7,5},{8,10},{9,11},{10,... | collective-permute-start | bytes 196616 | tf_op jit(solution)/shard_map/ppermute | solution.py:377
  7.9 4.2 %collective-permute-start.3 = (bf16[192,128]{1,0:T(8,128)(2,1)S(1)}, bf16[192,128]{1,0:T(8,128)(2,1)S(1)}, u32[]{:S(2)}, u32[]{:S(2)}) collective-permute-start(bf16[192,128]{1,0:T(8,128)(2,1)S(1)} %get-tuple-element.31), channel_id=1, source_target_pairs={{0,8},{8,0},{1,9},{9,1},{2,10},{10,2},{3,11},{11,3},{4,12},{12,4},... | collective-permute-start | bytes 147464 | tf_op jit(solution)/shard_map/ppermute | solution.py:371
  12.5 4.7 %collective-permute-start.7 = (bf16[64,768]{1,0:T(8,128)(2,1)S(1)}, bf16[64,768]{1,0:T(8,128)(2,1)S(1)}, u32[]{:S(2)}, u32[]{:S(2)}) collective-permute-start(bf16[64,768]{1,0:T(8,128)(2,1)S(1)} %get-tuple-element.33.refs_3_.refs_0_), channel_id=1, source_target_pairs={{0,8},{8,0},{1,9},{9,1},{2,10},{10,2},{3,11},{11,3},{4,12},{12,4},... | collective-permute-start | bytes 294920 | tf_op jit(solution)/shard_map/ppermute | solution.py:371
  14.1 1.6 %collective-permute-start.4 = (bf16[64,768]{1,0:T(8,128)(2,1)S(1)}, bf16[64,768]{1,0:T(8,128)(2,1)S(1)}, u32[]{:S(2)}, u32[]{:S(2)}) collective-permute-start(bf16[64,768]{1,0:T(8,128)(2,1)S(1)} %get-tuple-element.33.refs_3_.refs_0_), channel_id=1, source_target_pairs={{0,1},{1,0},{2,3},{3,2},{4,5},{5,4},{6,7},{7,6},{8,9},{9,8},{10,11... | collective-permute-start | bytes 294920 | tf_op jit(solution)/shard_map/ppermute | solution.py:397
  15.7 6.7 %collective-permute-start.6 = (bf16[64,1280]{1,0:T(8,128)(2,1)S(1)}, bf16[64,1280]{1,0:T(8,128)(2,1)S(1)}, u32[]{:S(2)}, u32[]{:S(2)}) collective-permute-start(bf16[64,1280]{1,0:T(8,128)(2,1)S(1)} %rest.1.refs_0_), channel_id=1, source_target_pairs={{0,8},{8,0},{1,9},{9,1},{2,10},{10,2},{3,11},{11,3},{4,12},{12,4},... | collective-permute-start | bytes 491528 | tf_op jit(solution)/shard_map/ppermute | solution.py:371
  17.2 1.3 %collective-permute-start.8 = (bf16[64,768]{1,0:T(8,128)(2,1)S(1)}, bf16[64,768]{1,0:T(8,128)(2,1)S(1)}, u32[]{:S(2)}, u32[]{:S(2)}) collective-permute-start(bf16[64,768]{1,0:T(8,128)(2,1)S(1)} %collective-permute-done.7.refs_2_), channel_id=1, source_target_pairs={{0,1},{1,0},{2,3},{3,2},{4,5},{5,4},{6,7},{7,6},{8,9},{9,8},{10,11... | collective-permute-start | bytes 294920 | tf_op jit(solution)/shard_map/ppermute | solution.py:402
  19.1 9.8 %collective-permute-start.10 = (bf16[192,768]{1,0:T(8,128)(2,1)S(1)}, bf16[192,768]{1,0:T(8,128)(2,1)S(1)}, u32[]{:S(2)}, u32[]{:S(2)}) collective-permute-start(bf16[192,768]{1,0:T(8,128)(2,1)S(1)} %get-tuple-element.41), channel_id=1, source_target_pairs={{0,16},{16,0},{1,17},{17,1},{2,18},{18,2},{3,19},{19,3},{4,20},{20... | collective-permute-start | bytes 884744 | tf_op jit(solution)/shard_map/ppermute | solution.py:371
  20.7 1.8 %collective-permute-start.5 = (bf16[64,1280]{1,0:T(8,128)(2,1)S(1)}, bf16[64,1280]{1,0:T(8,128)(2,1)S(1)}, u32[]{:S(2)}, u32[]{:S(2)}) collective-permute-start(bf16[64,1280]{1,0:T(8,128)(2,1)S(1)} %rest.1.refs_0_), channel_id=1, source_target_pairs={{0,1},{1,0},{2,3},{3,2},{4,5},{5,4},{6,7},{7,6},{8,9},{9,8},{10,11... | collective-permute-start | bytes 491528 | tf_op jit(solution)/shard_map/ppermute | solution.py:397
  22.4 1.4 %collective-permute-start.9 = (bf16[64,1280]{1,0:T(8,128)(2,1)S(1)}, bf16[64,1280]{1,0:T(8,128)(2,1)S(1)}, u32[]{:S(2)}, u32[]{:S(2)}) collective-permute-start(bf16[64,1280]{1,0:T(8,128)(2,1)S(1)} %collective-permute-done.6.refs_2_), channel_id=1, source_target_pairs={{0,1},{1,0},{2,3},{3,2},{4,5},{5,4},{6,7},{7,6},{8,9},{9,8},{10,11... | collective-permute-start | bytes 491528 | tf_op jit(solution)/shard_map/ppermute | solution.py:402
  24.7 4.2 %collective-permute-start.11 = (bf16[192,128]{1,0:T(8,128)(2,1)S(1)}, bf16[192,128]{1,0:T(8,128)(2,1)S(1)}, u32[]{:S(2)}, u32[]{:S(2)}) collective-permute-start(bf16[192,128]{1,0:T(8,128)(2,1)S(1)} %get-tuple-element.44), channel_id=1, source_target_pairs={{0,8},{8,0},{1,9},{9,1},{2,10},{10,2},{3,11},{11,3},{4,12},{12,4},... | collective-permute-start | bytes 147464 | tf_op jit(solution)/shard_map/ppermute | solution.py:371
  25.3 3.6 %copy-start = (f32[1,192,1024]{2,1,0:T(8,128)S(1)}, f32[1,192,1024]{2,1,0:T(8,128)}, u32[]{:S(2)}) copy-start(f32[1,192,1024]{2,1,0:T(8,128)} %param.13) | copy-start | bytes 2359300
  25.3 3.6 %copy-start.1 = (f32[1,192,1024]{2,1,0:T(8,128)S(1)}, f32[1,192,1024]{2,1,0:T(8,128)}, u32[]{:S(2)}) copy-start(f32[1,192,1024]{2,1,0:T(8,128)} %param.14) | copy-start | bytes 2359300
  25.3 5.1 %collective-permute-start.12 = (bf16[192,256]{1,0:T(8,128)(2,1)S(1)}, bf16[192,256]{1,0:T(8,128)(2,1)S(1)}, u32[]{:S(2)}, u32[]{:S(2)}) collective-permute-start(bf16[192,256]{1,0:T(8,128)(2,1)S(1)} %get-tuple-element.47), channel_id=1, source_target_pairs={{0,16},{16,0},{1,17},{17,1},{2,18},{18,2},{3,19},{19,3},{4,20},{20... | collective-permute-start | bytes 294920 | tf_op jit(solution)/shard_map/ppermute | solution.py:371
where the time goes:
time: 31.3 us; the launch traced here: 31.1 us
  starting transfers between devices  13.1 us (42%)
  waiting for transfers between devices  9.86 us (32%)
  Pallas kernels  7.49 us (24%)
  between operations  0.74 us (2%)
    ppermute x6, starting transfers between devices, ring(): lax.ppermute(value, name, [(k, (k + shift) % size) for k in range(size)])  7.36 us
    ppermute x6, waiting for transfers between devices, ring(): lax.ppermute(value, name, [(k, (k + shift) % size) for k in range(size)])  6.71 us
    pallas_call x10, Pallas kernels, call(): pl.pallas_call(body, out_shape=out_shape, in_specs=in_specs or [VMEM] * l...  6.09 us
    ppermute x3, starting transfers between devices, per_device(): arrived.append(lax.ppermute(blocks[k], 'expert', perm))  5.68 us
    ppermute x2, waiting for transfers between devices, spread(): quarters += [value, lax.ppermute(value, 'expert', swap)]  2.69 us
    pallas_call x1, Pallas kernels, pack_rows(): pl.pallas_call(functools.partial(pack_body, experts, n_island), out_shape...  1.39 us
  transfers between devices with their start and end apart: 13, of which 9 were waited for; matrix products, arithmetic and copies ran while one was open for 0% of the time, Pallas kernels for 17%

commit v1 on v0

--- a/solution.py
+++ b/solution.py
@@ -232,20 +232,19 @@
         out[...] = update(left_ref[...], slots_ref[:, at], state_refs, columns)
 
 
-def two_body(n_dp, n_island, pairs, *refs):
-    quarters = refs[: 2 * n_dp]
-    left_ref, *state_refs = refs[2 * n_dp : 2 * n_dp + 4]
-    *outs, slots_ref = refs[2 * n_dp + 4 :]
+def two_body(n_island, slots_ref, left_ref, *refs):
+    state_refs, outs = refs[:3], refs[-(n_island - 1) :]
     width = state_refs[0].shape[1]
     first = width - slots_ref.shape[1]
-    gather_slots(n_dp, pairs, quarters, slots_ref)
     places = pieces(n_island, width)[n_island - 1 :]
     for out, (at, columns) in zip(outs, places):
         slots = slots_ref[:, at.start - first : at.stop - first]
         out[...] = update(left_ref[...], slots, state_refs, columns)
 
 
-def hidden_body(n_dp, n_island, one_ref, two_ref, theta_ref, *outs):
+def hidden_body(n_dp, n_island, pairs, *refs):
+    one_ref, theta_ref, *outs, two_ref = refs[2 * n_dp :]
+    gather_slots(n_dp, pairs, refs[: 2 * n_dp], two_ref)
     data = lax.axis_index("dp")
     split = one_ref.shape[1]
     length = one_ref.shape[0] // n_dp
@@ -427,20 +426,19 @@
     )
     theirs = [ring(value, "island", n_island, shift + 1) for shift, value in enumerate(one)]
     two_quarters = spread(two_mine, left)
-    *two, two_slots = call(
-        functools.partial(two_body, n_dp, n_island, pairs),
-        [bf16((units, part - first))] * (n_island - 1)
-        + [bf16((n_dp * length, width - split))],
-        two_quarters + [left, *states],
+    *hidden, two_slots = call(
+        functools.partial(hidden_body, n_dp, n_island, pairs),
+        [bf16((units, length))] * n_dp + [bf16((n_dp * length, width - split))],
+        two_quarters + [one_slots, states[0]],
+        "hidden_grad",
+    )
+    two = call(
+        functools.partial(two_body, n_island),
+        [bf16((units, part - first))] * (n_island - 1),
+        [two_slots, left, *states, hidden[0]],
         "far_two",
     )
     theirs += [ring(value, "island", n_island, shift + 1) for shift, value in enumerate(two)]
-    hidden = call(
-        functools.partial(hidden_body, n_dp, n_island),
-        [bf16((units, length))] * n_dp,
-        [one_slots, two_slots, states[0]],
-        "hidden_grad",
-    )
     hidden = [hidden[0]] + [ring(hidden[s], "dp", n_dp, s) for s in range(1, n_dp)]
     (own,) = call(near_body, [bf16((units, part))], [two_slots, left, *states], "near_update")
     outer = [anchor.reshape(units, part), momentum.reshape(units, part), own]

time: 31.3 us -> 31.3 us (level)
  no operation moved by 1% of the time
where the time goes in v1:
time: 31.3 us; the launch traced here: 31.1 us
  starting transfers between devices  13.1 us (42%)
  waiting for transfers between devices  9.78 us (31%)
  Pallas kernels  7.48 us (24%)
  between operations  0.75 us (2%)
    ppermute x6, starting transfers between devices, ring(): lax.ppermute(value, name, [(k, (k + shift) % size) for k in range(size)])  7.43 us
    ppermute x6, waiting for transfers between devices, ring(): lax.ppermute(value, name, [(k, (k + shift) % size) for k in range(size)])  6.64 us
    pallas_call x10, Pallas kernels, call(): pl.pallas_call(body, out_shape=out_shape, in_specs=in_specs or [VMEM] * l...  6.08 us
    ppermute x3, starting transfers between devices, per_device(): arrived.append(lax.ppermute(blocks[k], 'expert', perm))  5.68 us
    ppermute x2, waiting for transfers between devices, spread(): quarters += [value, lax.ppermute(value, 'expert', swap)]  2.69 us
    pallas_call x1, Pallas kernels, pack_rows(): pl.pallas_call(functools.partial(pack_body, experts, n_island), out_shape...  1.39 us
  transfers between devices with their start and end apart: 13, of which 9 were waited for; matrix products, arithmetic and copies ran while one was open for 0% of the time, Pallas kernels for 17%

profile of v1, /device:TPU:0, one launch (start us, length us, event | category | flops | bytes accessed | tf_op | source)
XLA Modules:
  0.0 31.1 jit_solution(6594127513006704926)
XLA Ops:
  0.6 0.0 copy-start.2
  0.6 1.4 %pack.1 = (bf16[16,2048]{1,0:T(8,128)(2,1)S(1)}, bf16[16,2048]{1,0:T(8,128)(2,1)S(1)}, bf16[16,2048]{1,0:T(8,128)(2,1)S(1)}, bf16[16,2048]{1,0:T(8,128)(2,1)S(1)}) custom-call(s32[8,128]{1,0:T(8,128)} %bitcast.16, f32[8,128]{1,0:T(8,128)} %bitcast.17, s32[1,4]{1,0:T(1,128)} %counts_hbm.1, bf16[128,2048]{1,0:T(8,128)(2,1)} %cot_hbm.1), custom_call_target="tpu_custom_call" | custom-call | tf_op jit(solution)/shard_map/pack/pallas_call | solution.py:135
  2.0 4.1 %collective-permute-start = (bf16[16,2048]{1,0:T(8,128)(2,1)S(1)}, bf16[16,2048]{1,0:T(8,128)(2,1)S(1)}, u32[]{:S(2)}, u32[]{:S(2)}) collective-permute-start(bf16[16,2048]{1,0:T(8,128)(2,1)S(1)} %get-tuple-element.26), channel_id=1, source_target_pairs={{0,4},{1,5},{2,6},{3,7},{4,0},{5,1},{6,2},{7,3},{8,12},{9,13},{10,... | collective-permute-start | bytes 196616 | tf_op jit(solution)/shard_map/ppermute | solution.py:376
  6.1 1.3 %collective-permute-start.1 = (bf16[16,2048]{1,0:T(8,128)(2,1)S(1)}, bf16[16,2048]{1,0:T(8,128)(2,1)S(1)}, u32[]{:S(2)}, u32[]{:S(2)}) collective-permute-start(bf16[16,2048]{1,0:T(8,128)(2,1)S(1)} %get-tuple-element.27), channel_id=1, source_target_pairs={{0,6},{1,7},{2,4},{3,5},{4,2},{5,3},{6,0},{7,1},{8,14},{9,15},{10,... | collective-permute-start | bytes 196616 | tf_op jit(solution)/shard_map/ppermute | solution.py:376
  7.5 0.2 collective-permute-start.2
  7.7 0.0 copy-done.2
  7.7 0.1 split.1
  7.9 1.6 %collective-permute-start.3 = (bf16[192,128]{1,0:T(8,128)(2,1)S(1)}, bf16[192,128]{1,0:T(8,128)(2,1)S(1)}, u32[]{:S(2)}, u32[]{:S(2)}) collective-permute-start(bf16[192,128]{1,0:T(8,128)(2,1)S(1)} %get-tuple-element.30), channel_id=1, source_target_pairs={{0,8},{8,0},{1,9},{9,1},{2,10},{10,2},{3,11},{11,3},{4,12},{12,4},... | collective-permute-start | bytes 147464 | tf_op jit(solution)/shard_map/ppermute | solution.py:370
  9.4 2.6 %collective-permute-done.3.refs_4_.refs_5_ = bf16[192,128]{1,0:T(8,128)(2,1)S(1)} collective-permute-done((bf16[192,128]{1,0:T(8,128)(2,1)S(1)}, bf16[192,128]{1,0:T(8,128)(2,1)S(1)}, u32[]{:S(2)}, u32[]{:S(2)}) %collective-permute-start.3) | collective-permute-done | bytes 49184 | tf_op jit(solution)/shard_map/ppermute | solution.py:370
  12.0 0.0 collective-permute-done.refs_0_
  12.0 0.4 %collective-permute-done.1.refs_1_ = bf16[16,2048]{1,0:T(8,128)(2,1)S(1)} collective-permute-done((bf16[16,2048]{1,0:T(8,128)(2,1)S(1)}, bf16[16,2048]{1,0:T(8,128)(2,1)S(1)}, u32[]{:S(2)}, u32[]{:S(2)}) %collective-permute-start.1) | collective-permute-done | bytes 65568 | tf_op jit(solution)/shard_map/ppermute | solution.py:376
  12.4 0.1 collective-permute-done.2.refs_2_
  12.5 1.6 %collective-permute-start.7 = (bf16[64,768]{1,0:T(8,128)(2,1)S(1)}, bf16[64,768]{1,0:T(8,128)(2,1)S(1)}, u32[]{:S(2)}, u32[]{:S(2)}) collective-permute-start(bf16[64,768]{1,0:T(8,128)(2,1)S(1)} %get-tuple-element.32.refs_3_.refs_0_), channel_id=1, source_target_pairs={{0,8},{8,0},{1,9},{9,1},{2,10},{10,2},{3,11},{11,3},{4,12},{12,4},... | collective-permute-start | bytes 294920 | tf_op jit(solution)/shard_map/ppermute | solution.py:370
  14.1 0.0 collective-permute-start.4
  14.1 1.6 %stage.1 = (bf16[192,2048]{1,0:T(8,128)(2,1)S(1)}, bf16[192,2048]{1,0:T(8,128)(2,1)S(1)}, bf16[192,2048]{1,0:T(8,128)(2,1)S(1)}) custom-call(bf16[192,2048]{1,0:T(8,128)(2,1)} %bitcast.18, bf16[192,2048]{1,0:T(8,128)(2,1)} %bitcast.19, bf16[192,2048]{1,0:T(8,128)(2,1)} %bitcast.20, bf16[64,768]{1,0:T(8,128)(2,1)S(1)} %get-tuple-element.32.refs_3_.refs_0_), custom_call_target="tpu_custom_call" | custom-call | flops 1840000000 | tf_op jit(solution)/shard_map/stage/pallas_call | solution.py:335
  15.7 0.0 collective-permute-done.4.refs_0_.refs_1_
  15.7 0.6 %collective-permute-start.6 = (bf16[64,1280]{1,0:T(8,128)(2,1)S(1)}, bf16[64,1280]{1,0:T(8,128)(2,1)S(1)}, u32[]{:S(2)}, u32[]{:S(2)}) collective-permute-start(bf16[64,1280]{1,0:T(8,128)(2,1)S(1)} %rest.1.refs_0_), channel_id=1, source_target_pairs={{0,8},{8,0},{1,9},{9,1},{2,10},{10,2},{3,11},{11,3},{4,12},{12,4},... | collective-permute-start | bytes 491528 | tf_op jit(solution)/shard_map/ppermute | solution.py:370
  16.3 0.8 %collective-permute-done.7.refs_2_ = bf16[64,768]{1,0:T(8,128)(2,1)S(1)} collective-permute-done((bf16[64,768]{1,0:T(8,128)(2,1)S(1)}, bf16[64,768]{1,0:T(8,128)(2,1)S(1)}, u32[]{:S(2)}, u32[]{:S(2)}) %collective-permute-start.7) | collective-permute-done | bytes 98336 | tf_op jit(solution)/shard_map/ppermute | solution.py:370
  17.2 0.0 collective-permute-start.8
  17.2 1.3 %collective-permute-done.8.refs_3_ = bf16[64,768]{1,0:T(8,128)(2,1)S(1)} collective-permute-done((bf16[64,768]{1,0:T(8,128)(2,1)S(1)}, bf16[64,768]{1,0:T(8,128)(2,1)S(1)}, u32[]{:S(2)}, u32[]{:S(2)}) %collective-permute-start.8) | collective-permute-done | bytes 98336 | tf_op jit(solution)/shard_map/ppermute | solution.py:401
  18.5 0.6 %far_one.1 = (bf16[192,768]{1,0:T(8,128)(2,1)S(1)}, bf16[256,768]{1,0:T(8,128)(2,1)S(1)}, bf16[192,256]{1,0:T(8,128)(2,1)S(1)}) custom-call(bf16[64,768]{1,0:T(8,128)(2,1)S(1)} %get-tuple-element.32.refs_3_.refs_0_, bf16[64,768]{1,0:T(8,128)(2,1)S(1)} %collective-permute-done.4.refs_0_.refs_1_, bf16[64,768]{1,0:T(8,128)(2,1)S(1)} %collective-permute-done.7.refs_2_, ...), custom_call_target="tpu_custom_call" | custom-call | flops 115000000 | tf_op jit(solution)/shard_map/far_one/pallas_call | solution.py:335
  19.1 1.6 %collective-permute-start.10 = (bf16[192,768]{1,0:T(8,128)(2,1)S(1)}, bf16[192,768]{1,0:T(8,128)(2,1)S(1)}, u32[]{:S(2)}, u32[]{:S(2)}) collective-permute-start(bf16[192,768]{1,0:T(8,128)(2,1)S(1)} %get-tuple-element.41), channel_id=1, source_target_pairs={{0,16},{16,0},{1,17},{17,1},{2,18},{18,2},{3,19},{19,3},{4,20},{20... | collective-permute-start | bytes 884744 | tf_op jit(solution)/shard_map/ppermute | solution.py:370
  20.7 0.0 collective-permute-start.5
  20.7 1.8 %collective-permute-done.6.refs_2_ = bf16[64,1280]{1,0:T(8,128)(2,1)S(1)} collective-permute-done((bf16[64,1280]{1,0:T(8,128)(2,1)S(1)}, bf16[64,1280]{1,0:T(8,128)(2,1)S(1)}, u32[]{:S(2)}, u32[]{:S(2)}) %collective-permute-start.6) | collective-permute-done | bytes 163872 | tf_op jit(solution)/shard_map/ppermute | solution.py:370
  22.4 0.0 collective-permute-start.9
  22.4 0.0 collective-permute-done.5.refs_1_
  22.4 1.4 %collective-permute-done.9.refs_3_ = bf16[64,1280]{1,0:T(8,128)(2,1)S(1)} collective-permute-done((bf16[64,1280]{1,0:T(8,128)(2,1)S(1)}, bf16[64,1280]{1,0:T(8,128)(2,1)S(1)}, u32[]{:S(2)}, u32[]{:S(2)}) %collective-permute-start.9) | collective-permute-done | bytes 163872 | tf_op jit(solution)/shard_map/ppermute | solution.py:401
  23.8 0.6 %hidden_grad.1 = (bf16[192,128]{1,0:T(8,128)(2,1)S(1)}, bf16[192,128]{1,0:T(8,128)(2,1)S(1)}, bf16[256,1280]{1,0:T(8,128)(2,1)S(1)}) custom-call(bf16[64,1280]{1,0:T(8,128)(2,1)S(1)} %rest.1.refs_0_, bf16[64,1280]{1,0:T(8,128)(2,1)S(1)} %collective-permute-done.5.refs_1_, bf16[64,1280]{1,0:T(8,128)(2,1)S(1)} %collective-permute-done.6.refs_2_, ...), custom_call_target="tpu_custom_call" | custom-call | flops 345000000 | tf_op jit(solution)/shard_map/hidden_grad/pallas_call | solution.py:335
  24.4 0.6 %collective-permute-start.11 = (bf16[192,128]{1,0:T(8,128)(2,1)S(1)}, bf16[192,128]{1,0:T(8,128)(2,1)S(1)}, u32[]{:S(2)}, u32[]{:S(2)}) collective-permute-start(bf16[192,128]{1,0:T(8,128)(2,1)S(1)} %get-tuple-element.43), channel_id=1, source_target_pairs={{0,8},{8,0},{1,9},{9,1},{2,10},{10,2},{3,11},{11,3},{4,12},{12,4},... | collective-permute-start | bytes 147464 | tf_op jit(solution)/shard_map/ppermute | solution.py:370
  25.0 0.3 far_two.1
  25.3 0.0 copy-start
  25.3 0.0 copy-start.1
  25.3 1.6 %collective-permute-start.12 = (bf16[192,256]{1,0:T(8,128)(2,1)S(1)}, bf16[192,256]{1,0:T(8,128)(2,1)S(1)}, u32[]{:S(2)}, u32[]{:S(2)}) collective-permute-start(bf16[192,256]{1,0:T(8,128)(2,1)S(1)} %far_two.1), channel_id=1, source_target_pairs={{0,16},{16,0},{1,17},{17,1},{2,18},{18,2},{3,19},{19,3},{4,20},{20... | collective-permute-start | bytes 294920 | tf_op jit(solution)/shard_map/ppermute | solution.py:370
  26.8 0.7 %near_update.1.own_ref = bf16[192,1024]{1,0:T(8,128)(2,1)S(1)} custom-call(bf16[256,1280]{1,0:T(8,128)(2,1)S(1)} %get-tuple-element.40.slots_ref, bf16[192,256]{1,0:T(8,128)(2,1)S(1)} %get-tuple-element.37.left_ref, bf16[192,2048]{1,0:T(8,128)(2,1)S(1)} %get-tuple-element.33.refs_1_.refs_6_.refs_5_.refs_0_, ...), custom_call_target="tpu_custom_call" | custom-call | flops 345000000 | tf_op jit(solution)/shard_map/near_update/pallas_call | solution.py:335
  27.6 1.0 %collective-permute-done.11.refs_2_ = bf16[192,128]{1,0:T(8,128)(2,1)S(1)} collective-permute-done((bf16[192,128]{1,0:T(8,128)(2,1)S(1)}, bf16[192,128]{1,0:T(8,128)(2,1)S(1)}, u32[]{:S(2)}, u32[]{:S(2)}) %collective-permute-start.11) | collective-permute-done | bytes 49184 | tf_op jit(solution)/shard_map/ppermute | solution.py:370
  28.6 0.0 collective-permute-done.10.refs_0_
  28.6 0.0 copy-done
  28.6 0.0 copy-done.1
  28.6 1.3 %outer_one.1 = (f32[192,1024]{1,0:T(8,128)}, f32[192,1024]{1,0:T(8,128)}, bf16[128,384]{1,0:T(8,128)(2,1)}) custom-call(f32[192,1024]{1,0:T(8,128)S(1)} %bitcast.11, f32[192,1024]{1,0:T(8,128)S(1)} %bitcast.13, bf16[192,1024]{1,0:T(8,128)(2,1)S(1)} %near_update.1.own_ref, bf16[192,768]{1,0:T(8,128)(2,1)S(1)} %collective-permute-done.10.refs_0_, ...), custom_call_target="tpu_custom_call" | custom-call | flops 1264999936 | tf_op jit(solution)/shard_map/outer_one/pallas_call | solution.py:335
  29.9 0.4 %collective-permute-done.12.refs_0_ = bf16[192,256]{1,0:T(8,128)(2,1)S(1)} collective-permute-done((bf16[192,256]{1,0:T(8,128)(2,1)S(1)}, bf16[192,256]{1,0:T(8,128)(2,1)S(1)}, u32[]{:S(2)}, u32[]{:S(2)}) %collective-permute-start.12) | collective-permute-done | bytes 98336 | tf_op jit(solution)/shard_map/ppermute | solution.py:370
  30.3 0.8 %outer_two.1 = (f32[192,1024]{1,0:T(8,128)}, f32[192,1024]{1,0:T(8,128)}) custom-call(f32[192,1024]{1,0:T(8,128)} %get-tuple-element.44._, f32[192,1024]{1,0:T(8,128)} %get-tuple-element.45.__, f32[192,1024]{1,0:T(8,128)S(1)} %bitcast.12, f32[192,1024]{1,0:T(8,128)S(1)} %bitcast.14, ...), custom_call_target="tpu_custom_call", output_to_operand_aliasing={{0}: (0, {}), {1}: (1, {})} | custom-call | flops 1035000000 | tf_op jit(solution)/shard_map/outer_two/pallas_call | solution.py:335
  (2 shorter events, 0.0 us)
Async XLA Ops:
  0.6 7.1 %copy-start.2 = (bf16[1,1,1,128,384]{4,3,2,1,0:T(8,128)(2,1)S(1)}, bf16[1,1,1,128,384]{4,3,2,1,0:T(8,128)(2,1)}, u32[]{:S(2)}) copy-start(bf16[1,1,1,128,384]{4,3,2,1,0:T(8,128)(2,1)} %param.19) | copy-start | bytes 294916
  2.0 10.0 %collective-permute-start = (bf16[16,2048]{1,0:T(8,128)(2,1)S(1)}, bf16[16,2048]{1,0:T(8,128)(2,1)S(1)}, u32[]{:S(2)}, u32[]{:S(2)}) collective-permute-start(bf16[16,2048]{1,0:T(8,128)(2,1)S(1)} %get-tuple-element.26), channel_id=1, source_target_pairs={{0,4},{1,5},{2,6},{3,7},{4,0},{5,1},{6,2},{7,3},{8,12},{9,13},{10,... | collective-permute-start | bytes 196616 | tf_op jit(solution)/shard_map/ppermute | solution.py:376
  6.1 6.2 %collective-permute-start.1 = (bf16[16,2048]{1,0:T(8,128)(2,1)S(1)}, bf16[16,2048]{1,0:T(8,128)(2,1)S(1)}, u32[]{:S(2)}, u32[]{:S(2)}) collective-permute-start(bf16[16,2048]{1,0:T(8,128)(2,1)S(1)} %get-tuple-element.27), channel_id=1, source_target_pairs={{0,6},{1,7},{2,4},{3,5},{4,2},{5,3},{6,0},{7,1},{8,14},{9,15},{10,... | collective-permute-start | bytes 196616 | tf_op jit(solution)/shard_map/ppermute | solution.py:376
  7.5 5.0 %collective-permute-start.2 = (bf16[16,2048]{1,0:T(8,128)(2,1)S(1)}, bf16[16,2048]{1,0:T(8,128)(2,1)S(1)}, u32[]{:S(2)}, u32[]{:S(2)}) collective-permute-start(bf16[16,2048]{1,0:T(8,128)(2,1)S(1)} %get-tuple-element.28), channel_id=1, source_target_pairs={{0,2},{1,3},{2,0},{3,1},{4,6},{5,7},{6,4},{7,5},{8,10},{9,11},{10,... | collective-permute-start | bytes 196616 | tf_op jit(solution)/shard_map/ppermute | solution.py:376
  7.9 4.2 %collective-permute-start.3 = (bf16[192,128]{1,0:T(8,128)(2,1)S(1)}, bf16[192,128]{1,0:T(8,128)(2,1)S(1)}, u32[]{:S(2)}, u32[]{:S(2)}) collective-permute-start(bf16[192,128]{1,0:T(8,128)(2,1)S(1)} %get-tuple-element.30), channel_id=1, source_target_pairs={{0,8},{8,0},{1,9},{9,1},{2,10},{10,2},{3,11},{11,3},{4,12},{12,4},... | collective-permute-start | bytes 147464 | tf_op jit(solution)/shard_map/ppermute | solution.py:370
  12.5 4.7 %collective-permute-start.7 = (bf16[64,768]{1,0:T(8,128)(2,1)S(1)}, bf16[64,768]{1,0:T(8,128)(2,1)S(1)}, u32[]{:S(2)}, u32[]{:S(2)}) collective-permute-start(bf16[64,768]{1,0:T(8,128)(2,1)S(1)} %get-tuple-element.32.refs_3_.refs_0_), channel_id=1, source_target_pairs={{0,8},{8,0},{1,9},{9,1},{2,10},{10,2},{3,11},{11,3},{4,12},{12,4},... | collective-permute-start | bytes 294920 | tf_op jit(solution)/shard_map/ppermute | solution.py:370
  14.1 1.6 %collective-permute-start.4 = (bf16[64,768]{1,0:T(8,128)(2,1)S(1)}, bf16[64,768]{1,0:T(8,128)(2,1)S(1)}, u32[]{:S(2)}, u32[]{:S(2)}) collective-permute-start(bf16[64,768]{1,0:T(8,128)(2,1)S(1)} %get-tuple-element.32.refs_3_.refs_0_), channel_id=1, source_target_pairs={{0,1},{1,0},{2,3},{3,2},{4,5},{5,4},{6,7},{7,6},{8,9},{9,8},{10,11... | collective-permute-start | bytes 294920 | tf_op jit(solution)/shard_map/ppermute | solution.py:396
  15.7 6.7 %collective-permute-start.6 = (bf16[64,1280]{1,0:T(8,128)(2,1)S(1)}, bf16[64,1280]{1,0:T(8,128)(2,1)S(1)}, u32[]{:S(2)}, u32[]{:S(2)}) collective-permute-start(bf16[64,1280]{1,0:T(8,128)(2,1)S(1)} %rest.1.refs_0_), channel_id=1, source_target_pairs={{0,8},{8,0},{1,9},{9,1},{2,10},{10,2},{3,11},{11,3},{4,12},{12,4},... | collective-permute-start | bytes 491528 | tf_op jit(solution)/shard_map/ppermute | solution.py:370
  17.2 1.3 %collective-permute-start.8 = (bf16[64,768]{1,0:T(8,128)(2,1)S(1)}, bf16[64,768]{1,0:T(8,128)(2,1)S(1)}, u32[]{:S(2)}, u32[]{:S(2)}) collective-permute-start(bf16[64,768]{1,0:T(8,128)(2,1)S(1)} %collective-permute-done.7.refs_2_), channel_id=1, source_target_pairs={{0,1},{1,0},{2,3},{3,2},{4,5},{5,4},{6,7},{7,6},{8,9},{9,8},{10,11... | collective-permute-start | bytes 294920 | tf_op jit(solution)/shard_map/ppermute | solution.py:401
  19.1 9.5 %collective-permute-start.10 = (bf16[192,768]{1,0:T(8,128)(2,1)S(1)}, bf16[192,768]{1,0:T(8,128)(2,1)S(1)}, u32[]{:S(2)}, u32[]{:S(2)}) collective-permute-start(bf16[192,768]{1,0:T(8,128)(2,1)S(1)} %get-tuple-element.41), channel_id=1, source_target_pairs={{0,16},{16,0},{1,17},{17,1},{2,18},{18,2},{3,19},{19,3},{4,20},{20... | collective-permute-start | bytes 884744 | tf_op jit(solution)/shard_map/ppermute | solution.py:370
  20.7 1.8 %collective-permute-start.5 = (bf16[64,1280]{1,0:T(8,128)(2,1)S(1)}, bf16[64,1280]{1,0:T(8,128)(2,1)S(1)}, u32[]{:S(2)}, u32[]{:S(2)}) collective-permute-start(bf16[64,1280]{1,0:T(8,128)(2,1)S(1)} %rest.1.refs_0_), channel_id=1, source_target_pairs={{0,1},{1,0},{2,3},{3,2},{4,5},{5,4},{6,7},{7,6},{8,9},{9,8},{10,11... | collective-permute-start | bytes 491528 | tf_op jit(solution)/shard_map/ppermute | solution.py:396
  22.4 1.4 %collective-permute-start.9 = (bf16[64,1280]{1,0:T(8,128)(2,1)S(1)}, bf16[64,1280]{1,0:T(8,128)(2,1)S(1)}, u32[]{:S(2)}, u32[]{:S(2)}) collective-permute-start(bf16[64,1280]{1,0:T(8,128)(2,1)S(1)} %collective-permute-done.6.refs_2_), channel_id=1, source_target_pairs={{0,1},{1,0},{2,3},{3,2},{4,5},{5,4},{6,7},{7,6},{8,9},{9,8},{10,11... | collective-permute-start | bytes 491528 | tf_op jit(solution)/shard_map/ppermute | solution.py:401
  24.4 4.2 %collective-permute-start.11 = (bf16[192,128]{1,0:T(8,128)(2,1)S(1)}, bf16[192,128]{1,0:T(8,128)(2,1)S(1)}, u32[]{:S(2)}, u32[]{:S(2)}) collective-permute-start(bf16[192,128]{1,0:T(8,128)(2,1)S(1)} %get-tuple-element.43), channel_id=1, source_target_pairs={{0,8},{8,0},{1,9},{9,1},{2,10},{10,2},{3,11},{11,3},{4,12},{12,4},... | collective-permute-start | bytes 147464 | tf_op jit(solution)/shard_map/ppermute | solution.py:370
  25.3 3.3 %copy-start = (f32[1,192,1024]{2,1,0:T(8,128)S(1)}, f32[1,192,1024]{2,1,0:T(8,128)}, u32[]{:S(2)}) copy-start(f32[1,192,1024]{2,1,0:T(8,128)} %param.13) | copy-start | bytes 2359300
  25.3 3.3 %copy-start.1 = (f32[1,192,1024]{2,1,0:T(8,128)S(1)}, f32[1,192,1024]{2,1,0:T(8,128)}, u32[]{:S(2)}) copy-start(f32[1,192,1024]{2,1,0:T(8,128)} %param.14) | copy-start | bytes 2359300
  25.3 5.1 %collective-permute-start.12 = (bf16[192,256]{1,0:T(8,128)(2,1)S(1)}, bf16[192,256]{1,0:T(8,128)(2,1)S(1)}, u32[]{:S(2)}, u32[]{:S(2)}) collective-permute-start(bf16[192,256]{1,0:T(8,128)(2,1)S(1)} %far_two.1), channel_id=1, source_target_pairs={{0,16},{16,0},{1,17},{17,1},{2,18},{18,2},{3,19},{19,3},{4,20},{20... | collective-permute-start | bytes 294920 | tf_op jit(solution)/shard_map/ppermute | solution.py:370

commit v2 on v1

--- a/solution.py
+++ b/solution.py
@@ -91,7 +91,7 @@
             ]
         )
     ]
-    for copy in copies:
+    for copy in copies[3:] + copies[:3]:
         copy.start()
     width, tokens = ids_ref.shape
     rows = experts * CAP

time: 31.3 us -> 31.3 us (level)
  no operation moved by 1% of the time
where the time goes in v2:
time: 31.3 us; the launch traced here: 31.2 us
  starting transfers between devices  13.1 us (42%)
  waiting for transfers between devices  9.79 us (31%)
  Pallas kernels  7.49 us (24%)
  between operations  0.75 us (2%)
    ppermute x6, starting transfers between devices, ring(): lax.ppermute(value, name, [(k, (k + shift) % size) for k in range(size)])  7.42 us
    ppermute x6, waiting for transfers between devices, ring(): lax.ppermute(value, name, [(k, (k + shift) % size) for k in range(size)])  6.65 us
    pallas_call x10, Pallas kernels, call(): pl.pallas_call(body, out_shape=out_shape, in_specs=in_specs or [VMEM] * l...  6.08 us
    ppermute x3, starting transfers between devices, per_device(): arrived.append(lax.ppermute(blocks[k], 'expert', perm))  5.68 us
    ppermute x2, waiting for transfers between devices, spread(): quarters += [value, lax.ppermute(value, 'expert', swap)]  2.69 us
    pallas_call x1, Pallas kernels, pack_rows(): pl.pallas_call(functools.partial(pack_body, experts, n_island), out_shape...  1.41 us
  transfers between devices with their start and end apart: 13, of which 9 were waited for; matrix products, arithmetic and copies ran while one was open for 0% of the time, Pallas kernels for 17%

profile of v2, /device:TPU:0, one launch (start us, length us, event | category | flops | bytes accessed | tf_op | source)
XLA Modules:
  0.0 31.2 jit_solution(1118947679394589853)
XLA Ops:
  0.6 0.0 copy-start.2
  0.6 1.4 %pack.1 = (bf16[16,2048]{1,0:T(8,128)(2,1)S(1)}, bf16[16,2048]{1,0:T(8,128)(2,1)S(1)}, bf16[16,2048]{1,0:T(8,128)(2,1)S(1)}, bf16[16,2048]{1,0:T(8,128)(2,1)S(1)}) custom-call(s32[8,128]{1,0:T(8,128)} %bitcast.16, f32[8,128]{1,0:T(8,128)} %bitcast.17, s32[1,4]{1,0:T(1,128)} %counts_hbm.1, bf16[128,2048]{1,0:T(8,128)(2,1)} %cot_hbm.1), custom_call_target="tpu_custom_call" | custom-call | tf_op jit(solution)/shard_map/pack/pallas_call | solution.py:135
  2.1 4.1 %collective-permute-start = (bf16[16,2048]{1,0:T(8,128)(2,1)S(1)}, bf16[16,2048]{1,0:T(8,128)(2,1)S(1)}, u32[]{:S(2)}, u32[]{:S(2)}) collective-permute-start(bf16[16,2048]{1,0:T(8,128)(2,1)S(1)} %get-tuple-element.26), channel_id=1, source_target_pairs={{0,4},{1,5},{2,6},{3,7},{4,0},{5,1},{6,2},{7,3},{8,12},{9,13},{10,... | collective-permute-start | bytes 196616 | tf_op jit(solution)/shard_map/ppermute | solution.py:376
  6.2 1.4 %collective-permute-start.1 = (bf16[16,2048]{1,0:T(8,128)(2,1)S(1)}, bf16[16,2048]{1,0:T(8,128)(2,1)S(1)}, u32[]{:S(2)}, u32[]{:S(2)}) collective-permute-start(bf16[16,2048]{1,0:T(8,128)(2,1)S(1)} %get-tuple-element.27), channel_id=1, source_target_pairs={{0,6},{1,7},{2,4},{3,5},{4,2},{5,3},{6,0},{7,1},{8,14},{9,15},{10,... | collective-permute-start | bytes 196616 | tf_op jit(solution)/shard_map/ppermute | solution.py:376
  7.5 0.2 collective-permute-start.2
  7.7 0.0 copy-done.2
  7.7 0.1 split.1
  7.9 1.6 %collective-permute-start.3 = (bf16[192,128]{1,0:T(8,128)(2,1)S(1)}, bf16[192,128]{1,0:T(8,128)(2,1)S(1)}, u32[]{:S(2)}, u32[]{:S(2)}) collective-permute-start(bf16[192,128]{1,0:T(8,128)(2,1)S(1)} %get-tuple-element.30), channel_id=1, source_target_pairs={{0,8},{8,0},{1,9},{9,1},{2,10},{10,2},{3,11},{11,3},{4,12},{12,4},... | collective-permute-start | bytes 147464 | tf_op jit(solution)/shard_map/ppermute | solution.py:370
  9.5 2.6 %collective-permute-done.3.refs_4_.refs_5_ = bf16[192,128]{1,0:T(8,128)(2,1)S(1)} collective-permute-done((bf16[192,128]{1,0:T(8,128)(2,1)S(1)}, bf16[192,128]{1,0:T(8,128)(2,1)S(1)}, u32[]{:S(2)}, u32[]{:S(2)}) %collective-permute-start.3) | collective-permute-done | bytes 49184 | tf_op jit(solution)/shard_map/ppermute | solution.py:370
  12.0 0.0 collective-permute-done.refs_0_
  12.0 0.4 %collective-permute-done.1.refs_1_ = bf16[16,2048]{1,0:T(8,128)(2,1)S(1)} collective-permute-done((bf16[16,2048]{1,0:T(8,128)(2,1)S(1)}, bf16[16,2048]{1,0:T(8,128)(2,1)S(1)}, u32[]{:S(2)}, u32[]{:S(2)}) %collective-permute-start.1) | collective-permute-done | bytes 65568 | tf_op jit(solution)/shard_map/ppermute | solution.py:376
  12.4 0.1 collective-permute-done.2.refs_2_
  12.5 1.6 %collective-permute-start.7 = (bf16[64,768]{1,0:T(8,128)(2,1)S(1)}, bf16[64,768]{1,0:T(8,128)(2,1)S(1)}, u32[]{:S(2)}, u32[]{:S(2)}) collective-permute-start(bf16[64,768]{1,0:T(8,128)(2,1)S(1)} %get-tuple-element.32.refs_3_.refs_0_), channel_id=1, source_target_pairs={{0,8},{8,0},{1,9},{9,1},{2,10},{10,2},{3,11},{11,3},{4,12},{12,4},... | collective-permute-start | bytes 294920 | tf_op jit(solution)/shard_map/ppermute | solution.py:370
  14.1 0.0 collective-permute-start.4
  14.1 1.6 %stage.1 = (bf16[192,2048]{1,0:T(8,128)(2,1)S(1)}, bf16[192,2048]{1,0:T(8,128)(2,1)S(1)}, bf16[192,2048]{1,0:T(8,128)(2,1)S(1)}) custom-call(bf16[192,2048]{1,0:T(8,128)(2,1)} %bitcast.18, bf16[192,2048]{1,0:T(8,128)(2,1)} %bitcast.19, bf16[192,2048]{1,0:T(8,128)(2,1)} %bitcast.20, bf16[64,768]{1,0:T(8,128)(2,1)S(1)} %get-tuple-element.32.refs_3_.refs_0_), custom_call_target="tpu_custom_call" | custom-call | flops 1840000000 | tf_op jit(solution)/shard_map/stage/pallas_call | solution.py:335
  15.7 0.0 collective-permute-done.4.refs_0_.refs_1_
  15.8 0.6 %collective-permute-start.6 = (bf16[64,1280]{1,0:T(8,128)(2,1)S(1)}, bf16[64,1280]{1,0:T(8,128)(2,1)S(1)}, u32[]{:S(2)}, u32[]{:S(2)}) collective-permute-start(bf16[64,1280]{1,0:T(8,128)(2,1)S(1)} %rest.1.refs_0_), channel_id=1, source_target_pairs={{0,8},{8,0},{1,9},{9,1},{2,10},{10,2},{3,11},{11,3},{4,12},{12,4},... | collective-permute-start | bytes 491528 | tf_op jit(solution)/shard_map/ppermute | solution.py:370
  16.3 0.8 %collective-permute-done.7.refs_2_ = bf16[64,768]{1,0:T(8,128)(2,1)S(1)} collective-permute-done((bf16[64,768]{1,0:T(8,128)(2,1)S(1)}, bf16[64,768]{1,0:T(8,128)(2,1)S(1)}, u32[]{:S(2)}, u32[]{:S(2)}) %collective-permute-start.7) | collective-permute-done | bytes 98336 | tf_op jit(solution)/shard_map/ppermute | solution.py:370
  17.2 0.0 collective-permute-start.8
  17.2 1.3 %collective-permute-done.8.refs_3_ = bf16[64,768]{1,0:T(8,128)(2,1)S(1)} collective-permute-done((bf16[64,768]{1,0:T(8,128)(2,1)S(1)}, bf16[64,768]{1,0:T(8,128)(2,1)S(1)}, u32[]{:S(2)}, u32[]{:S(2)}) %collective-permute-start.8) | collective-permute-done | bytes 98336 | tf_op jit(solution)/shard_map/ppermute | solution.py:401
  18.5 0.6 %far_one.1 = (bf16[192,768]{1,0:T(8,128)(2,1)S(1)}, bf16[256,768]{1,0:T(8,128)(2,1)S(1)}, bf16[192,256]{1,0:T(8,128)(2,1)S(1)}) custom-call(bf16[64,768]{1,0:T(8,128)(2,1)S(1)} %get-tuple-element.32.refs_3_.refs_0_, bf16[64,768]{1,0:T(8,128)(2,1)S(1)} %collective-permute-done.4.refs_0_.refs_1_, bf16[64,768]{1,0:T(8,128)(2,1)S(1)} %collective-permute-done.7.refs_2_, ...), custom_call_target="tpu_custom_call" | custom-call | flops 115000000 | tf_op jit(solution)/shard_map/far_one/pallas_call | solution.py:335
  19.1 1.6 %collective-permute-start.10 = (bf16[192,768]{1,0:T(8,128)(2,1)S(1)}, bf16[192,768]{1,0:T(8,128)(2,1)S(1)}, u32[]{:S(2)}, u32[]{:S(2)}) collective-permute-start(bf16[192,768]{1,0:T(8,128)(2,1)S(1)} %get-tuple-element.41), channel_id=1, source_target_pairs={{0,16},{16,0},{1,17},{17,1},{2,18},{18,2},{3,19},{19,3},{4,20},{20... | collective-permute-start | bytes 884744 | tf_op jit(solution)/shard_map/ppermute | solution.py:370
  20.7 0.0 collective-permute-start.5
  20.7 1.8 %collective-permute-done.6.refs_2_ = bf16[64,1280]{1,0:T(8,128)(2,1)S(1)} collective-permute-done((bf16[64,1280]{1,0:T(8,128)(2,1)S(1)}, bf16[64,1280]{1,0:T(8,128)(2,1)S(1)}, u32[]{:S(2)}, u32[]{:S(2)}) %collective-permute-start.6) | collective-permute-done | bytes 163872 | tf_op jit(solution)/shard_map/ppermute | solution.py:370
  22.4 0.0 collective-permute-start.9
  22.4 0.0 collective-permute-done.5.refs_1_
  22.4 1.4 %collective-permute-done.9.refs_3_ = bf16[64,1280]{1,0:T(8,128)(2,1)S(1)} collective-permute-done((bf16[64,1280]{1,0:T(8,128)(2,1)S(1)}, bf16[64,1280]{1,0:T(8,128)(2,1)S(1)}, u32[]{:S(2)}, u32[]{:S(2)}) %collective-permute-start.9) | collective-permute-done | bytes 163872 | tf_op jit(solution)/shard_map/ppermute | solution.py:401
  23.8 0.6 %hidden_grad.1 = (bf16[192,128]{1,0:T(8,128)(2,1)S(1)}, bf16[192,128]{1,0:T(8,128)(2,1)S(1)}, bf16[256,1280]{1,0:T(8,128)(2,1)S(1)}) custom-call(bf16[64,1280]{1,0:T(8,128)(2,1)S(1)} %rest.1.refs_0_, bf16[64,1280]{1,0:T(8,128)(2,1)S(1)} %collective-permute-done.5.refs_1_, bf16[64,1280]{1,0:T(8,128)(2,1)S(1)} %collective-permute-done.6.refs_2_, ...), custom_call_target="tpu_custom_call" | custom-call | flops 345000000 | tf_op jit(solution)/shard_map/hidden_grad/pallas_call | solution.py:335
  24.4 0.6 %collective-permute-start.11 = (bf16[192,128]{1,0:T(8,128)(2,1)S(1)}, bf16[192,128]{1,0:T(8,128)(2,1)S(1)}, u32[]{:S(2)}, u32[]{:S(2)}) collective-permute-start(bf16[192,128]{1,0:T(8,128)(2,1)S(1)} %get-tuple-element.43), channel_id=1, source_target_pairs={{0,8},{8,0},{1,9},{9,1},{2,10},{10,2},{3,11},{11,3},{4,12},{12,4},... | collective-permute-start | bytes 147464 | tf_op jit(solution)/shard_map/ppermute | solution.py:370
  25.0 0.3 far_two.1
  25.3 0.0 copy-start
  25.3 0.0 copy-start.1
  25.3 1.6 %collective-permute-start.12 = (bf16[192,256]{1,0:T(8,128)(2,1)S(1)}, bf16[192,256]{1,0:T(8,128)(2,1)S(1)}, u32[]{:S(2)}, u32[]{:S(2)}) collective-permute-start(bf16[192,256]{1,0:T(8,128)(2,1)S(1)} %far_two.1), channel_id=1, source_target_pairs={{0,16},{16,0},{1,17},{17,1},{2,18},{18,2},{3,19},{19,3},{4,20},{20... | collective-permute-start | bytes 294920 | tf_op jit(solution)/shard_map/ppermute | solution.py:370
  26.9 0.7 %near_update.1.own_ref = bf16[192,1024]{1,0:T(8,128)(2,1)S(1)} custom-call(bf16[256,1280]{1,0:T(8,128)(2,1)S(1)} %get-tuple-element.40.slots_ref, bf16[192,256]{1,0:T(8,128)(2,1)S(1)} %get-tuple-element.37.left_ref, bf16[192,2048]{1,0:T(8,128)(2,1)S(1)} %get-tuple-element.33.refs_1_.refs_6_.refs_5_.refs_0_, ...), custom_call_target="tpu_custom_call" | custom-call | flops 345000000 | tf_op jit(solution)/shard_map/near_update/pallas_call | solution.py:335
  27.6 1.0 %collective-permute-done.11.refs_2_ = bf16[192,128]{1,0:T(8,128)(2,1)S(1)} collective-permute-done((bf16[192,128]{1,0:T(8,128)(2,1)S(1)}, bf16[192,128]{1,0:T(8,128)(2,1)S(1)}, u32[]{:S(2)}, u32[]{:S(2)}) %collective-permute-start.11) | collective-permute-done | bytes 49184 | tf_op jit(solution)/shard_map/ppermute | solution.py:370
  28.6 0.0 collective-permute-done.10.refs_0_
  28.6 0.0 copy-done
  28.6 0.0 copy-done.1
  28.6 1.3 %outer_one.1 = (f32[192,1024]{1,0:T(8,128)}, f32[192,1024]{1,0:T(8,128)}, bf16[128,384]{1,0:T(8,128)(2,1)}) custom-call(f32[192,1024]{1,0:T(8,128)S(1)} %bitcast.11, f32[192,1024]{1,0:T(8,128)S(1)} %bitcast.13, bf16[192,1024]{1,0:T(8,128)(2,1)S(1)} %near_update.1.own_ref, bf16[192,768]{1,0:T(8,128)(2,1)S(1)} %collective-permute-done.10.refs_0_, ...), custom_call_target="tpu_custom_call" | custom-call | flops 1264999936 | tf_op jit(solution)/shard_map/outer_one/pallas_call | solution.py:335
  29.9 0.4 %collective-permute-done.12.refs_0_ = bf16[192,256]{1,0:T(8,128)(2,1)S(1)} collective-permute-done((bf16[192,256]{1,0:T(8,128)(2,1)S(1)}, bf16[192,256]{1,0:T(8,128)(2,1)S(1)}, u32[]{:S(2)}, u32[]{:S(2)}) %collective-permute-start.12) | collective-permute-done | bytes 98336 | tf_op jit(solution)/shard_map/ppermute | solution.py:370
  30.4 0.8 %outer_two.1 = (f32[192,1024]{1,0:T(8,128)}, f32[192,1024]{1,0:T(8,128)}) custom-call(f32[192,1024]{1,0:T(8,128)} %get-tuple-element.44._, f32[192,1024]{1,0:T(8,128)} %get-tuple-element.45.__, f32[192,1024]{1,0:T(8,128)S(1)} %bitcast.12, f32[192,1024]{1,0:T(8,128)S(1)} %bitcast.14, ...), custom_call_target="tpu_custom_call", output_to_operand_aliasing={{0}: (0, {}), {1}: (1, {})} | custom-call | flops 1035000000 | tf_op jit(solution)/shard_map/outer_two/pallas_call | solution.py:335
  (2 shorter events, 0.0 us)
Async XLA Ops:
  0.6 7.1 %copy-start.2 = (bf16[1,1,1,128,384]{4,3,2,1,0:T(8,128)(2,1)S(1)}, bf16[1,1,1,128,384]{4,3,2,1,0:T(8,128)(2,1)}, u32[]{:S(2)}) copy-start(bf16[1,1,1,128,384]{4,3,2,1,0:T(8,128)(2,1)} %param.19) | copy-start | bytes 294916
  2.1 10.0 %collective-permute-start = (bf16[16,2048]{1,0:T(8,128)(2,1)S(1)}, bf16[16,2048]{1,0:T(8,128)(2,1)S(1)}, u32[]{:S(2)}, u32[]{:S(2)}) collective-permute-start(bf16[16,2048]{1,0:T(8,128)(2,1)S(1)} %get-tuple-element.26), channel_id=1, source_target_pairs={{0,4},{1,5},{2,6},{3,7},{4,0},{5,1},{6,2},{7,3},{8,12},{9,13},{10,... | collective-permute-start | bytes 196616 | tf_op jit(solution)/shard_map/ppermute | solution.py:376
  6.2 6.2 %collective-permute-start.1 = (bf16[16,2048]{1,0:T(8,128)(2,1)S(1)}, bf16[16,2048]{1,0:T(8,128)(2,1)S(1)}, u32[]{:S(2)}, u32[]{:S(2)}) collective-permute-start(bf16[16,2048]{1,0:T(8,128)(2,1)S(1)} %get-tuple-element.27), channel_id=1, source_target_pairs={{0,6},{1,7},{2,4},{3,5},{4,2},{5,3},{6,0},{7,1},{8,14},{9,15},{10,... | collective-permute-start | bytes 196616 | tf_op jit(solution)/shard_map/ppermute | solution.py:376
  7.5 5.0 %collective-permute-start.2 = (bf16[16,2048]{1,0:T(8,128)(2,1)S(1)}, bf16[16,2048]{1,0:T(8,128)(2,1)S(1)}, u32[]{:S(2)}, u32[]{:S(2)}) collective-permute-start(bf16[16,2048]{1,0:T(8,128)(2,1)S(1)} %get-tuple-element.28), channel_id=1, source_target_pairs={{0,2},{1,3},{2,0},{3,1},{4,6},{5,7},{6,4},{7,5},{8,10},{9,11},{10,... | collective-permute-start | bytes 196616 | tf_op jit(solution)/shard_map/ppermute | solution.py:376
  7.9 4.2 %collective-permute-start.3 = (bf16[192,128]{1,0:T(8,128)(2,1)S(1)}, bf16[192,128]{1,0:T(8,128)(2,1)S(1)}, u32[]{:S(2)}, u32[]{:S(2)}) collective-permute-start(bf16[192,128]{1,0:T(8,128)(2,1)S(1)} %get-tuple-element.30), channel_id=1, source_target_pairs={{0,8},{8,0},{1,9},{9,1},{2,10},{10,2},{3,11},{11,3},{4,12},{12,4},... | collective-permute-start | bytes 147464 | tf_op jit(solution)/shard_map/ppermute | solution.py:370
  12.5 4.7 %collective-permute-start.7 = (bf16[64,768]{1,0:T(8,128)(2,1)S(1)}, bf16[64,768]{1,0:T(8,128)(2,1)S(1)}, u32[]{:S(2)}, u32[]{:S(2)}) collective-permute-start(bf16[64,768]{1,0:T(8,128)(2,1)S(1)} %get-tuple-element.32.refs_3_.refs_0_), channel_id=1, source_target_pairs={{0,8},{8,0},{1,9},{9,1},{2,10},{10,2},{3,11},{11,3},{4,12},{12,4},... | collective-permute-start | bytes 294920 | tf_op jit(solution)/shard_map/ppermute | solution.py:370
  14.1 1.6 %collective-permute-start.4 = (bf16[64,768]{1,0:T(8,128)(2,1)S(1)}, bf16[64,768]{1,0:T(8,128)(2,1)S(1)}, u32[]{:S(2)}, u32[]{:S(2)}) collective-permute-start(bf16[64,768]{1,0:T(8,128)(2,1)S(1)} %get-tuple-element.32.refs_3_.refs_0_), channel_id=1, source_target_pairs={{0,1},{1,0},{2,3},{3,2},{4,5},{5,4},{6,7},{7,6},{8,9},{9,8},{10,11... | collective-permute-start | bytes 294920 | tf_op jit(solution)/shard_map/ppermute | solution.py:396
  15.8 6.7 %collective-permute-start.6 = (bf16[64,1280]{1,0:T(8,128)(2,1)S(1)}, bf16[64,1280]{1,0:T(8,128)(2,1)S(1)}, u32[]{:S(2)}, u32[]{:S(2)}) collective-permute-start(bf16[64,1280]{1,0:T(8,128)(2,1)S(1)} %rest.1.refs_0_), channel_id=1, source_target_pairs={{0,8},{8,0},{1,9},{9,1},{2,10},{10,2},{3,11},{11,3},{4,12},{12,4},... | collective-permute-start | bytes 491528 | tf_op jit(solution)/shard_map/ppermute | solution.py:370
  17.2 1.3 %collective-permute-start.8 = (bf16[64,768]{1,0:T(8,128)(2,1)S(1)}, bf16[64,768]{1,0:T(8,128)(2,1)S(1)}, u32[]{:S(2)}, u32[]{:S(2)}) collective-permute-start(bf16[64,768]{1,0:T(8,128)(2,1)S(1)} %collective-permute-done.7.refs_2_), channel_id=1, source_target_pairs={{0,1},{1,0},{2,3},{3,2},{4,5},{5,4},{6,7},{7,6},{8,9},{9,8},{10,11... | collective-permute-start | bytes 294920 | tf_op jit(solution)/shard_map/ppermute | solution.py:401
  19.1 9.5 %collective-permute-start.10 = (bf16[192,768]{1,0:T(8,128)(2,1)S(1)}, bf16[192,768]{1,0:T(8,128)(2,1)S(1)}, u32[]{:S(2)}, u32[]{:S(2)}) collective-permute-start(bf16[192,768]{1,0:T(8,128)(2,1)S(1)} %get-tuple-element.41), channel_id=1, source_target_pairs={{0,16},{16,0},{1,17},{17,1},{2,18},{18,2},{3,19},{19,3},{4,20},{20... | collective-permute-start | bytes 884744 | tf_op jit(solution)/shard_map/ppermute | solution.py:370
  20.7 1.8 %collective-permute-start.5 = (bf16[64,1280]{1,0:T(8,128)(2,1)S(1)}, bf16[64,1280]{1,0:T(8,128)(2,1)S(1)}, u32[]{:S(2)}, u32[]{:S(2)}) collective-permute-start(bf16[64,1280]{1,0:T(8,128)(2,1)S(1)} %rest.1.refs_0_), channel_id=1, source_target_pairs={{0,1},{1,0},{2,3},{3,2},{4,5},{5,4},{6,7},{7,6},{8,9},{9,8},{10,11... | collective-permute-start | bytes 491528 | tf_op jit(solution)/shard_map/ppermute | solution.py:396
  22.4 1.4 %collective-permute-start.9 = (bf16[64,1280]{1,0:T(8,128)(2,1)S(1)}, bf16[64,1280]{1,0:T(8,128)(2,1)S(1)}, u32[]{:S(2)}, u32[]{:S(2)}) collective-permute-start(bf16[64,1280]{1,0:T(8,128)(2,1)S(1)} %collective-permute-done.6.refs_2_), channel_id=1, source_target_pairs={{0,1},{1,0},{2,3},{3,2},{4,5},{5,4},{6,7},{7,6},{8,9},{9,8},{10,11... | collective-permute-start | bytes 491528 | tf_op jit(solution)/shard_map/ppermute | solution.py:401
  24.4 4.2 %collective-permute-start.11 = (bf16[192,128]{1,0:T(8,128)(2,1)S(1)}, bf16[192,128]{1,0:T(8,128)(2,1)S(1)}, u32[]{:S(2)}, u32[]{:S(2)}) collective-permute-start(bf16[192,128]{1,0:T(8,128)(2,1)S(1)} %get-tuple-element.43), channel_id=1, source_target_pairs={{0,8},{8,0},{1,9},{9,1},{2,10},{10,2},{3,11},{11,3},{4,12},{12,4},... | collective-permute-start | bytes 147464 | tf_op jit(solution)/shard_map/ppermute | solution.py:370
  25.3 3.3 %copy-start = (f32[1,192,1024]{2,1,0:T(8,128)S(1)}, f32[1,192,1024]{2,1,0:T(8,128)}, u32[]{:S(2)}) copy-start(f32[1,192,1024]{2,1,0:T(8,128)} %param.13) | copy-start | bytes 2359300
  25.3 3.3 %copy-start.1 = (f32[1,192,1024]{2,1,0:T(8,128)S(1)}, f32[1,192,1024]{2,1,0:T(8,128)}, u32[]{:S(2)}) copy-start(f32[1,192,1024]{2,1,0:T(8,128)} %param.14) | copy-start | bytes 2359300
  25.3 5.1 %collective-permute-start.12 = (bf16[192,256]{1,0:T(8,128)(2,1)S(1)}, bf16[192,256]{1,0:T(8,128)(2,1)S(1)}, u32[]{:S(2)}, u32[]{:S(2)}) collective-permute-start(bf16[192,256]{1,0:T(8,128)(2,1)S(1)} %far_two.1), channel_id=1, source_target_pairs={{0,16},{16,0},{1,17},{17,1},{2,18},{18,2},{3,19},{19,3},{4,20},{20... | collective-permute-start | bytes 294920 | tf_op jit(solution)/shard_map/ppermute | solution.py:370
